TPU v7x, 32 devices: a whole 2x2x4 slice. The times are simulated.
32 devices in a mesh: ctx: 8 (over y, x, core), wsh: 4 (over z).
Axes of the slice: x: 2, y: 2, z: 4, core: 2. Of those that a mesh axis runs over, the one named last changes fastest.
Arguments:
- hidden_state: bfloat16 [12, 2048, 512], P('wsh', 'ctx'), may hold values from -1.6953125 to 1.6953125
- prev_state: bfloat16 [12, 2048, 512], P('wsh', 'ctx'), may hold values from -1.6953125 to 1.6953125
- halt_sum: float32 [12, 2048], P('wsh', 'ctx'), may hold values from 0 to 0.9
- halt_code: int32 [12, 2048], P('wsh', 'ctx'), may hold values from 0 to 2
- step_count: int32 [12, 2048], P('wsh', 'ctx'), may hold values from 0 to 3
- w_query: bfloat16 [512, 512], P(None, 'wsh'), may hold values from -0.25 to 0.25
- w_key: bfloat16 [512, 512], P(None, 'wsh'), may hold values from -0.25 to 0.25
- w_value: bfloat16 [512, 512], P(None, 'wsh'), may hold values from -0.25 to 0.25
- w_out: bfloat16 [512, 512], P('wsh'), may hold values from -2.5 to 2.5
- w_inner: bfloat16 [512, 2048], P(None, 'wsh'), may hold values from -0.25 to 0.25
- b_inner: bfloat16 [2048], P('wsh'), may hold values from -2.5 to 2.5
- w_outer: bfloat16 [2048, 512], P('wsh'), may hold values from -0.125 to 0.125
- b_outer: bfloat16 [512], P('wsh'), may hold values from -2.5 to 2.5
- gain_attention: bfloat16 [512], P('wsh'), may hold values from 0.099609375 to 1.8984375
- shift_attention: bfloat16 [512], P('wsh'), may hold values from -2.5 to 2.5
- gain_feedforward: bfloat16 [512], P('wsh'), may hold values from 0.099609375 to 1.8984375
- shift_feedforward: bfloat16 [512], P('wsh'), may hold values from -2.5 to 2.5
- w_halt: bfloat16 [512], P('wsh'), may hold values from -0.25 to 0.25
- b_halt: float32 [1], replicated, may hold values from -1 to 1
- grad_transformed: bfloat16 [12, 2048, 512], P('wsh', 'ctx'), may hold values from -1.6953125 to 1.6953125
- grad_blended: bfloat16 [12, 2048, 512], P('wsh', 'ctx'), may hold values from -1.6953125 to 1.6953125
- grad_sum: float32 [12, 2048], P('wsh', 'ctx'), may hold values from -1.7 to 1.7
Outputs:
- transformed: bfloat16 [12, 2048, 512], P('wsh', 'ctx')
- blended: bfloat16 [12, 2048, 512], P('wsh', 'ctx')
- new_sum: float32 [12, 2048], P('wsh', 'ctx')
- grad_state: float32 [12, 2048, 512], P('wsh', 'ctx')
- grad_prev: float32 [12, 2048, 512], P('wsh', 'ctx')
- grad_halt_sum: float32 [12, 2048], P('wsh', 'ctx')
- grad_w_query: float32 [512, 512], P(None, 'wsh')
- grad_w_key: float32 [512, 512], P(None, 'wsh')
- grad_w_value: float32 [512, 512], P(None, 'wsh')
- grad_w_out: float32 [512, 512], P('wsh')
- grad_w_inner: float32 [512, 2048], P(None, 'wsh')
- grad_b_inner: float32 [2048], P('wsh')
- grad_w_outer: float32 [2048, 512], P('wsh')
- grad_b_outer: float32 [512], P('wsh')
- grad_gain_attention: float32 [512], P('wsh')
- grad_shift_attention: float32 [512], P('wsh')
- grad_gain_feedforward: float32 [512], P('wsh')
- grad_shift_feedforward: float32 [512], P('wsh')
- grad_w_halt: float32 [512], P('wsh')
- grad_b_halt: float32 [1], replicated
Inputs may be any that keep to these rules, and one draw needn't show every extreme that they name: halt_code is 0 for a token that halted earlier, 1 for one that keeps running, 2 for one that halts at this step.
All inputs are finite; a program needn't handle non-finite values.
Results may differ from a plain program's by a relative error of at most 0.028.
Values may be sent and summed in bfloat16 or wider, within the bound.
No kernel may reach another device: no remote copies, remote signals or barrier semaphores. Data moves between devices by JAX's collectives and lax.ppermute only.
A program may use at most 320 MiB of HBM per device.

v0:
```python
import math

import jax
import jax.numpy as jnp
from jax import lax
from jax.sharding import PartitionSpec as P

HEADS = 8


epsilon = 1e-06
highest = lax.Precision.HIGHEST


def gelu_exact(values):
    return 0.5 * values * (1.0 + lax.erf(values * 2.0 ** (-0.5)))


def gelu_slope(values):
    return 0.5 * (1.0 + lax.erf(values * 2.0 ** (-0.5))) + values * jnp.exp(
        -0.5 * values * values
    ) * (2.0 * math.pi) ** (-0.5)


def signal(places, columns):
    halves = columns // 2
    frequency = jnp.exp(-math.log(10000.0) * jnp.arange(halves, dtype=jnp.float32) / (halves - 1))
    angles = places.astype(jnp.float32)[:, None] * frequency[None, :]
    return jnp.concatenate([jnp.sin(angles), jnp.cos(angles)], axis=1)


def norm_rows(summed, gain_row, shift_row):
    centre = summed - jnp.mean(summed, axis=1, keepdims=True)
    inverse = lax.rsqrt(jnp.mean(centre * centre, axis=1, keepdims=True) + epsilon)
    normed = centre * inverse
    return (normed * gain_row + shift_row, normed, inverse)


def norm_back(grad_out, normed, inverse, gain_row):
    scaled = grad_out * gain_row
    grad_in = inverse * (
        scaled
        - jnp.mean(scaled, axis=1, keepdims=True)
        - normed * jnp.mean(scaled * normed, axis=1, keepdims=True)
    )
    return (grad_in, jnp.sum(grad_out * normed, axis=0), jnp.sum(grad_out, axis=0))


def run_batch(
    gathered,
    position_code,
    state_rows,
    prev_rows,
    sum_rows,
    code_rows,
    count_rows,
    final_grad_rows,
    blend_grad_rows,
    sum_grad_rows,
    halt_offset,
):
    (
        query_full,
        key_full,
        value_full,
        out_full,
        inner_full,
        inner_bias,
        outer_full,
        outer_bias,
        gain_one,
        shift_one,
        gain_two,
        shift_two,
        halt_full,
    ) = gathered
    block_rows, model_width = state_rows.shape
    head_count = HEADS
    head_width = model_width // head_count
    score_scale = head_width ** (-0.5)
    gain_one_float = gain_one.astype(jnp.float32)
    gain_two_float = gain_two.astype(jnp.float32)
    embedded = state_rows.astype(jnp.float32) + position_code + signal(count_rows, model_width)
    halt_row = halt_full.astype(jnp.float32)
    halt_prob = jax.nn.sigmoid(jnp.dot(embedded, halt_row, precision=highest) + halt_offset[0])
    embed_low = embedded.astype(jnp.bfloat16)
    queries = jnp.dot(embed_low, query_full, preferred_element_type=jnp.float32).astype(
        jnp.bfloat16
    )
    keys_own = jnp.dot(embed_low, key_full, preferred_element_type=jnp.float32).astype(jnp.bfloat16)
    values_own = jnp.dot(embed_low, value_full, preferred_element_type=jnp.float32).astype(
        jnp.bfloat16
    )
    query_heads = queries.reshape(block_rows, head_count, head_width)
    start_fold = (
        jnp.zeros((block_rows, head_count, head_width), jnp.float32),
        jnp.full((head_count, block_rows), -jnp.inf, jnp.float32),
        jnp.zeros((head_count, block_rows), jnp.float32),
    )
    key_piece = lax.all_gather(keys_own, "ctx", axis=0, tiled=True)
    value_piece = lax.all_gather(values_own, "ctx", axis=0, tiled=True)
    piece_rows = key_piece.shape[0]
    stride = math.gcd(piece_rows, 512)

    def attend_sweep(number, inner_fold):
        weighted, row_peak, row_mass = inner_fold
        key_part = lax.dynamic_slice_in_dim(key_piece, number * stride, stride, 0).reshape(
            stride, head_count, head_width
        )
        value_part = lax.dynamic_slice_in_dim(value_piece, number * stride, stride, 0).reshape(
            stride, head_count, head_width
        )
        scores = (
            jnp.einsum("qhd,khd->hqk", query_heads, key_part, preferred_element_type=jnp.float32)
            * score_scale
        )
        top_now = jnp.maximum(row_peak, jnp.max(scores, axis=2))
        factor = jnp.exp(row_peak - top_now)
        exponent = jnp.exp(scores - top_now[:, :, None])
        row_mass = row_mass * factor + jnp.sum(exponent, axis=2)
        weighted = weighted * factor.T[:, :, None] + jnp.einsum(
            "hqk,khd->qhd",
            exponent.astype(jnp.bfloat16),
            value_part,
            preferred_element_type=jnp.float32,
        )
        return (weighted, top_now, row_mass)

    weighted, row_peak, row_mass = lax.fori_loop(0, piece_rows // stride, attend_sweep, start_fold)
    attended = weighted / row_mass.T[:, :, None]
    log_mass = row_peak + jnp.log(row_mass)
    attended_low = attended.reshape(block_rows, model_width).astype(jnp.bfloat16)
    branch = jnp.dot(attended_low, out_full, preferred_element_type=jnp.float32)
    norm_one, normed_one, inverse_one = norm_rows(
        embedded + branch, gain_one_float, shift_one.astype(jnp.float32)
    )
    norm_low = norm_one.astype(jnp.bfloat16)
    inner_pre = jnp.dot(
        norm_low, inner_full, preferred_element_type=jnp.float32
    ) + inner_bias.astype(jnp.float32)
    inner_low = gelu_exact(inner_pre).astype(jnp.bfloat16)
    feed_out = jnp.dot(
        inner_low, outer_full, preferred_element_type=jnp.float32
    ) + outer_bias.astype(jnp.float32)
    final, normed_two, inverse_two = norm_rows(
        norm_one + feed_out, gain_two_float, shift_two.astype(jnp.float32)
    )
    running = (code_rows > 0).astype(jnp.float32)
    halting = (code_rows == 2).astype(jnp.float32)
    update = running * (halting * (1.0 - sum_rows) + (1.0 - halting) * halt_prob)
    new_sum = sum_rows + update
    prev_float = prev_rows.astype(jnp.float32)
    blended = (prev_float * (1.0 - update)[:, None] + final * update[:, None]).astype(jnp.bfloat16)
    final_grad = final_grad_rows.astype(jnp.float32)
    blend_grad = blend_grad_rows.astype(jnp.float32)
    grad_update = jnp.sum(blend_grad * (final - prev_float), axis=1) + sum_grad_rows
    grad_prev = blend_grad * (1.0 - update)[:, None]
    grad_halt = sum_grad_rows - running * halting * grad_update
    grad_final = final_grad + update[:, None] * blend_grad
    grad_logit = grad_update * running * (1.0 - halting) * halt_prob * (1.0 - halt_prob)
    grad_halt_row = jnp.dot(grad_logit, embedded, precision=highest)
    grad_halt_bias = jnp.sum(grad_logit)
    grad_two, grad_gain_two, grad_shift_two = norm_back(
        grad_final, normed_two, inverse_two, gain_two_float
    )
    feed_grad_low = grad_two.astype(jnp.bfloat16)
    grad_outer_bias = jnp.sum(feed_grad_low.astype(jnp.float32), axis=0)
    grad_outer = jnp.einsum(
        "tf,td->fd", inner_low, feed_grad_low, preferred_element_type=jnp.float32
    )
    inner_back = jnp.einsum(
        "td,fd->tf", feed_grad_low, outer_full, preferred_element_type=jnp.float32
    )
    inner_grad_low = (inner_back * gelu_slope(inner_pre)).astype(jnp.bfloat16)
    grad_inner_bias = jnp.sum(inner_grad_low.astype(jnp.float32), axis=0)
    grad_inner = jnp.einsum(
        "td,tf->df", norm_low, inner_grad_low, preferred_element_type=jnp.float32
    )
    grad_norm_one = grad_two + jnp.einsum(
        "tf,df->td", inner_grad_low, inner_full, preferred_element_type=jnp.float32
    )
    grad_one, grad_gain_one, grad_shift_one = norm_back(
        grad_norm_one, normed_one, inverse_one, gain_one_float
    )
    branch_grad_low = grad_one.astype(jnp.bfloat16)
    grad_out_full = jnp.einsum(
        "td,te->de", attended_low, branch_grad_low, preferred_element_type=jnp.float32
    )
    attended_grad_low = jnp.einsum(
        "te,de->td", branch_grad_low, out_full, preferred_element_type=jnp.float32
    ).astype(jnp.bfloat16)
    grad_heads = attended_grad_low.reshape(block_rows, head_count, head_width)
    delta = jnp.sum(grad_heads.astype(jnp.float32) * attended, axis=2).T

    def score_grads(query_part, grad_part, key_part, value_part, mass_part, delta_part):
        scores = (
            jnp.einsum("qhd,khd->hqk", query_part, key_part, preferred_element_type=jnp.float32)
            * score_scale
        )
        probs = jnp.exp(scores - mass_part[:, :, None])
        grad_probs = jnp.einsum(
            "qhd,khd->hqk", grad_part, value_part, preferred_element_type=jnp.float32
        )
        return (probs, (probs * (grad_probs - delta_part[:, :, None])).astype(jnp.bfloat16))

    query_zeros = jnp.zeros((block_rows, head_count, head_width), jnp.float32)
    full_rows = block_rows * lax.axis_size("ctx")
    empty_fold = (
        query_zeros,
        jnp.zeros((full_rows, model_width), jnp.float32),
        jnp.zeros((full_rows, model_width), jnp.float32),
    )
    revisit_key_piece = lax.all_gather(keys_own, "ctx", axis=0, tiled=True)
    revisit_value_piece = lax.all_gather(values_own, "ctx", axis=0, tiled=True)
    piece_rows = revisit_key_piece.shape[0]
    revisit_stride = math.gcd(piece_rows, 512)

    def revisit_sweep(number, inner_fold):
        grad_queries, grad_keys, grad_values = inner_fold
        key_part = lax.dynamic_slice_in_dim(
            revisit_key_piece, number * revisit_stride, revisit_stride, 0
        ).reshape(revisit_stride, head_count, head_width)
        value_part = lax.dynamic_slice_in_dim(
            revisit_value_piece, number * revisit_stride, revisit_stride, 0
        ).reshape(revisit_stride, head_count, head_width)
        probs, grad_scores = score_grads(
            query_heads, grad_heads, key_part, value_part, log_mass, delta
        )
        grad_queries = grad_queries + score_scale * jnp.einsum(
            "hqk,khd->qhd", grad_scores, key_part, preferred_element_type=jnp.float32
        )
        fresh_keys = (
            score_scale
            * jnp.einsum(
                "hqk,qhd->khd", grad_scores, query_heads, preferred_element_type=jnp.float32
            )
        ).reshape(revisit_stride, model_width)
        fresh_values = jnp.einsum(
            "hqk,qhd->khd",
            probs.astype(jnp.bfloat16),
            grad_heads,
            preferred_element_type=jnp.float32,
        ).reshape(revisit_stride, model_width)
        offset = number * revisit_stride
        grad_keys = lax.dynamic_update_slice_in_dim(
            grad_keys,
            lax.dynamic_slice_in_dim(grad_keys, offset, revisit_stride, 0) + fresh_keys,
            offset,
            0,
        )
        grad_values = lax.dynamic_update_slice_in_dim(
            grad_values,
            lax.dynamic_slice_in_dim(grad_values, offset, revisit_stride, 0) + fresh_values,
            offset,
            0,
        )
        return (grad_queries, grad_keys, grad_values)

    grad_queries, grad_keys, grad_values = lax.fori_loop(
        0, piece_rows // revisit_stride, revisit_sweep, empty_fold
    )
    grad_key_rows, grad_value_rows = (
        lax.psum_scatter(
            grad_keys.astype(jnp.bfloat16), "ctx", scatter_dimension=0, tiled=True
        ).astype(jnp.float32),
        lax.psum_scatter(
            grad_values.astype(jnp.bfloat16), "ctx", scatter_dimension=0, tiled=True
        ).astype(jnp.float32),
    )
    query_grad_low = grad_queries.reshape(block_rows, model_width).astype(jnp.bfloat16)
    key_grad_low = grad_key_rows.astype(jnp.bfloat16)
    value_grad_low = grad_value_rows.astype(jnp.bfloat16)
    grad_query_full = jnp.einsum(
        "td,te->de", embed_low, query_grad_low, preferred_element_type=jnp.float32
    )
    grad_key_full = jnp.einsum(
        "td,te->de", embed_low, key_grad_low, preferred_element_type=jnp.float32
    )
    grad_value_full = jnp.einsum(
        "td,te->de", embed_low, value_grad_low, preferred_element_type=jnp.float32
    )
    grad_state = grad_one + grad_logit[:, None] * halt_row[None, :]
    grad_state = grad_state + jnp.einsum(
        "te,de->td", query_grad_low, query_full, preferred_element_type=jnp.float32
    )
    grad_state = grad_state + jnp.einsum(
        "te,de->td", key_grad_low, key_full, preferred_element_type=jnp.float32
    )
    grad_state = grad_state + jnp.einsum(
        "te,de->td", value_grad_low, value_full, preferred_element_type=jnp.float32
    )
    outputs = (final.astype(jnp.bfloat16), blended, new_sum, grad_state, grad_prev, grad_halt)
    grads = (
        grad_query_full,
        grad_key_full,
        grad_value_full,
        grad_out_full,
        grad_inner,
        grad_inner_bias,
        grad_outer,
        grad_outer_bias,
        grad_gain_one,
        grad_shift_one,
        grad_gain_two,
        grad_shift_two,
        grad_halt_row,
        grad_halt_bias,
    )
    return (outputs, grads)


def body(
    hidden_state,
    prev_state,
    halt_sum,
    halt_code,
    step_count,
    w_query,
    w_key,
    w_value,
    w_out,
    w_inner,
    b_inner,
    w_outer,
    b_outer,
    gain_attention,
    shift_attention,
    gain_feedforward,
    shift_feedforward,
    w_halt,
    b_halt,
    grad_transformed,
    grad_blended,
    grad_sum,
):
    batches, block_rows, model_width = hidden_state.shape
    places = lax.axis_index("ctx") * block_rows + jnp.arange(block_rows, dtype=jnp.int32)
    position_code = signal(places, model_width)
    collected = []
    summed = None
    for number in range(batches):
        gathered = (
            lax.all_gather(w_query, "wsh", axis=1, tiled=True),
            lax.all_gather(w_key, "wsh", axis=1, tiled=True),
            lax.all_gather(w_value, "wsh", axis=1, tiled=True),
            lax.all_gather(w_out, "wsh", axis=0, tiled=True),
            lax.all_gather(w_inner, "wsh", axis=1, tiled=True),
            lax.all_gather(b_inner, "wsh", axis=0, tiled=True),
            lax.all_gather(w_outer, "wsh", axis=0, tiled=True),
            lax.all_gather(b_outer, "wsh", axis=0, tiled=True),
            lax.all_gather(gain_attention, "wsh", axis=0, tiled=True),
            lax.all_gather(shift_attention, "wsh", axis=0, tiled=True),
            lax.all_gather(gain_feedforward, "wsh", axis=0, tiled=True),
            lax.all_gather(shift_feedforward, "wsh", axis=0, tiled=True),
            lax.all_gather(w_halt, "wsh", axis=0, tiled=True),
        )
        outputs, grads = run_batch(
            gathered,
            position_code,
            hidden_state[number],
            prev_state[number],
            halt_sum[number],
            halt_code[number],
            step_count[number],
            grad_transformed[number],
            grad_blended[number],
            grad_sum[number],
            b_halt,
        )
        collected.append(outputs)
        summed = grads if summed is None else jax.tree.map(jnp.add, summed, grads)
    stacked = [
        jnp.stack([record[column_index] for record in collected], axis=0)
        for column_index in range(6)
    ]
    bias_rows = jnp.full((lax.axis_size("wsh"),), summed[13], jnp.float32)
    shares = (
        lax.psum_scatter(
            summed[0].astype(jnp.bfloat16), "wsh", scatter_dimension=1, tiled=True
        ).astype(jnp.float32),
        lax.psum_scatter(
            summed[1].astype(jnp.bfloat16), "wsh", scatter_dimension=1, tiled=True
        ).astype(jnp.float32),
        lax.psum_scatter(
            summed[2].astype(jnp.bfloat16), "wsh", scatter_dimension=1, tiled=True
        ).astype(jnp.float32),
        lax.psum_scatter(
            summed[3].astype(jnp.bfloat16), "wsh", scatter_dimension=0, tiled=True
        ).astype(jnp.float32),
        lax.psum_scatter(
            summed[4].astype(jnp.bfloat16), "wsh", scatter_dimension=1, tiled=True
        ).astype(jnp.float32),
        lax.psum_scatter(
            summed[5].astype(jnp.bfloat16), "wsh", scatter_dimension=0, tiled=True
        ).astype(jnp.float32),
        lax.psum_scatter(
            summed[6].astype(jnp.bfloat16), "wsh", scatter_dimension=0, tiled=True
        ).astype(jnp.float32),
        lax.psum_scatter(
            summed[7].astype(jnp.bfloat16), "wsh", scatter_dimension=0, tiled=True
        ).astype(jnp.float32),
        lax.psum_scatter(
            summed[8].astype(jnp.bfloat16), "wsh", scatter_dimension=0, tiled=True
        ).astype(jnp.float32),
        lax.psum_scatter(
            summed[9].astype(jnp.bfloat16), "wsh", scatter_dimension=0, tiled=True
        ).astype(jnp.float32),
        lax.psum_scatter(
            summed[10].astype(jnp.bfloat16), "wsh", scatter_dimension=0, tiled=True
        ).astype(jnp.float32),
        lax.psum_scatter(
            summed[11].astype(jnp.bfloat16), "wsh", scatter_dimension=0, tiled=True
        ).astype(jnp.float32),
        lax.psum_scatter(
            summed[12].astype(jnp.bfloat16), "wsh", scatter_dimension=0, tiled=True
        ).astype(jnp.float32),
        lax.psum_scatter(
            bias_rows.astype(jnp.bfloat16), "wsh", scatter_dimension=0, tiled=True
        ).astype(jnp.float32),
    )
    totals = (
        lax.psum(shares[0].astype(jnp.bfloat16), "ctx").astype(jnp.float32),
        lax.psum(shares[1].astype(jnp.bfloat16), "ctx").astype(jnp.float32),
        lax.psum(shares[2].astype(jnp.bfloat16), "ctx").astype(jnp.float32),
        lax.psum(shares[3].astype(jnp.bfloat16), "ctx").astype(jnp.float32),
        lax.psum(shares[4].astype(jnp.bfloat16), "ctx").astype(jnp.float32),
        lax.psum(shares[5].astype(jnp.bfloat16), "ctx").astype(jnp.float32),
        lax.psum(shares[6].astype(jnp.bfloat16), "ctx").astype(jnp.float32),
        lax.psum(shares[7].astype(jnp.bfloat16), "ctx").astype(jnp.float32),
        lax.psum(shares[8].astype(jnp.bfloat16), "ctx").astype(jnp.float32),
        lax.psum(shares[9].astype(jnp.bfloat16), "ctx").astype(jnp.float32),
        lax.psum(shares[10].astype(jnp.bfloat16), "ctx").astype(jnp.float32),
        lax.psum(shares[11].astype(jnp.bfloat16), "ctx").astype(jnp.float32),
        lax.psum(shares[12].astype(jnp.bfloat16), "ctx").astype(jnp.float32),
        lax.psum(shares[13].astype(jnp.bfloat16), "ctx").astype(jnp.float32),
    )
    return (
        stacked[0],
        stacked[1],
        stacked[2],
        stacked[3],
        stacked[4],
        stacked[5],
        totals[0],
        totals[1],
        totals[2],
        totals[3],
        totals[4],
        totals[5],
        totals[6],
        totals[7],
        totals[8],
        totals[9],
        totals[10],
        totals[11],
        totals[12],
        totals[13],
    )


def solution(mesh):
    in_specs = (
        P("wsh", "ctx", None),
        P("wsh", "ctx", None),
        P("wsh", "ctx"),
        P("wsh", "ctx"),
        P("wsh", "ctx"),
        P(None, "wsh"),
        P(None, "wsh"),
        P(None, "wsh"),
        P("wsh", None),
        P(None, "wsh"),
        P("wsh"),
        P("wsh", None),
        P("wsh"),
        P("wsh"),
        P("wsh"),
        P("wsh"),
        P("wsh"),
        P("wsh"),
        P(),
        P("wsh", "ctx", None),
        P("wsh", "ctx", None),
        P("wsh", "ctx"),
    )
    out_specs = (
        P("wsh", "ctx", None),
        P("wsh", "ctx", None),
        P("wsh", "ctx"),
        P("wsh", "ctx", None),
        P("wsh", "ctx", None),
        P("wsh", "ctx"),
        P(None, "wsh"),
        P(None, "wsh"),
        P(None, "wsh"),
        P("wsh", None),
        P(None, "wsh"),
        P("wsh"),
        P("wsh", None),
        P("wsh"),
        P("wsh"),
        P("wsh"),
        P("wsh"),
        P("wsh"),
        P("wsh"),
        P(),
    )
    return jax.shard_map(body, mesh=mesh, in_specs=in_specs, out_specs=out_specs, check_vma=False)
```

profile of v0, /device:TPU:0, one launch (start us, length us, event | category | flops | bytes accessed | tf_op | source)
XLA Modules:
  0.0 968.9 jit_solution(8926064667089394260)
XLA Ops:
  8.1 16.9 %all_gather.38 = bf16[512,512]{1,0:T(8,128)(2,1)S(1)} all-gather(bf16[512,128]{1,0:T(8,128)(2,1)} %param.40), channel_id=1, replica_groups=mesh['ctx'=8,'wsh'=4] {'wsh'}, dimensions={1}, use_global_device_ids=true | all-gather | bytes 655360 | tf_op jit(solution)/shard_map/all_gather | solution.py:344
  25.0 3.7 multiply_sine_fusion.6
  31.2 14.6 %all_gather.41 = bf16[512,512]{1,0:T(8,128)(2,1)S(1)} all-gather(bf16[512,128]{1,0:T(8,128)(2,1)S(1)} %copy-done.105), channel_id=1, replica_groups=mesh['ctx'=8,'wsh'=4] {'wsh'}, dimensions={1}, use_global_device_ids=true | all-gather | bytes 655360 | tf_op jit(solution)/shard_map/all_gather | solution.py:345
  52.6 13.9 %all_gather.40 = bf16[512,512]{1,0:T(8,128)(2,1)S(1)} all-gather(bf16[512,128]{1,0:T(8,128)(2,1)S(1)} %copy-done.106), channel_id=1, replica_groups=mesh['ctx'=8,'wsh'=4] {'wsh'}, dimensions={1}, use_global_device_ids=true | all-gather | bytes 655360 | tf_op jit(solution)/shard_map/all_gather | solution.py:343
  69.8 15.5 %all_gather.43 = bf16[512,512]{1,0:T(8,128)(2,1)S(1)} all-gather(bf16[128,512]{1,0:T(8,128)(2,1)} %param.42), channel_id=1, replica_groups=mesh['ctx'=8,'wsh'=4] {'wsh'}, dimensions={0}, use_global_device_ids=true | all-gather | bytes 655360 | tf_op jit(solution)/shard_map/all_gather | solution.py:346
  85.4 9.8 %all-gather = bf16[4,1,128]{2,1,0:T(2,128)(2,1)S(1)} all-gather(bf16[1,1,128]{2,1,0:T(2,128)(2,1)S(1)} %bitcast.703), channel_id=1, replica_groups=mesh['ctx'=8,'wsh'=4] {'wsh'}, dimensions={0}, use_global_device_ids=true | all-gather | bytes 1280 | tf_op jit(solution)/shard_map/all_gather | solution.py:351
  95.1 7.5 all-gather.1
  102.7 11.9 %all-gather.2 = bf16[4,1,512]{2,1,0:T(2,128)(2,1)S(1)} all-gather(bf16[1,1,512]{2,1,0:T(2,128)(2,1)S(1)} %reshape.706), channel_id=1, replica_groups=mesh['ctx'=8,'wsh'=4] {'wsh'}, dimensions={0}, use_global_device_ids=true | all-gather | bytes 5120 | tf_op jit(solution)/shard_map/all_gather | solution.py:348
  114.6 8.6 all-gather.3
  125.4 8.4 all-gather.4
  133.8 8.6 all-gather.5
  142.4 8.6 all-gather.6
  155.4 4.0 copy.100
  159.4 4.0 copy.101
  163.4 34.1 %while.110 = (s32[]{:T(128)}, f32[256,8,64]{0,2,1:T(8,128)S(1)}, f32[8,256]{1,0:T(8,128)S(1)}, f32[8,256]{1,0:T(8,128)S(1)}, bf16[2048,512]{0,1:T(8,128)(2,1)}, ...) while((s32[]{:T(128)}, f32[256,8,64]{0,2,1:T(8,128)S(1)}, ...), condition=%wide.region_19.0_spmd.clone, body=%wide.region_16.19_spmd.clone.sunk | while | flops 277229568 | bytes 33947844 | solution.py:129
  200.2 4.0 copy.97
  204.2 4.0 copy.98
  208.1 34.1 %while.109 = (s32[]{:T(128)}, f32[256,8,64]{0,2,1:T(8,128)S(1)}, f32[8,256]{1,0:T(8,128)S(1)}, f32[8,256]{1,0:T(8,128)S(1)}, bf16[2048,512]{0,1:T(8,128)(2,1)}, ...) while((s32[]{:T(128)}, f32[256,8,64]{0,2,1:T(8,128)S(1)}, ...), condition=%wide.region_11.0_spmd.clone, body=%wide.region_8.11_spmd.clone.sunk | while | flops 277229568 | bytes 33947844 | solution.py:129
  242.2 4.2 copy.94
  246.4 3.7 convolution_add_fusion
  250.1 23.5 %all-gather.22.cloned.1.call-done = bf16[2048,512]{1,0:T(8,128)(2,1)} async-done(((bf16[512,512]{1,0:T(8,128)(2,1)}), bf16[2048,512]{1,0:T(8,128)(2,1)}) %all-gather.22.cloned.1.call-update) | async-done | bytes 2097168 | tf_op jit(solution)/shard_map/all_gather | solution.py:349
  282.3 20.5 %all-gather.18.cloned.1.call-done = bf16[2048,512]{1,0:T(8,128)(2,1)} async-done(((bf16[256,512]{1,0:T(8,128)(2,1)}), bf16[2048,512]{1,0:T(8,128)(2,1)}) %all-gather.18.cloned.1.call-update) | async-done | bytes 2097168 | tf_op jit(solution)/shard_map/all_gather | solution.py:101
  302.7 4.0 copy.95
  306.8 34.3 %while.108 = (s32[]{:T(128)}, f32[256,8,64]{0,2,1:T(8,128)S(1)}, f32[8,256]{1,0:T(8,128)S(1)}, f32[8,256]{1,0:T(8,128)S(1)}, bf16[2048,512]{0,1:T(8,128)(2,1)}, ...) while((s32[]{:T(128)}, f32[256,8,64]{0,2,1:T(8,128)S(1)}, ...), condition=%wide.region_3.0_spmd.clone, body=%wide.region_0.0_spmd.clone.sunk | while | flops 277229568 | bytes 33947844 | solution.py:129
  374.3 44.1 %while.111 = (s32[]{:T(128)}, f32[256,8,64]{0,2,1:T(8,128)}, f32[2048,512]{0,1:T(8,128)}, f32[2048,512]{0,1:T(8,128)}, bf16[2048,512]{0,1:T(8,128)(2,1)}, /*inde...) while((s32[]{:T(128)}, f32[256,8,64]{0,2,1:T(8,128)}, ...), condition=%wide.region_31.0_spmd.clone, body=%wide.region_30.0_spmd.clone.sunk | while | flops 680656896 | bytes 33054920 | solution.py:259
  380.0 3.3 constant_dynamic-update-slice_fusion.9
  418.4 3.9 convert_element_type.646
  429.1 44.5 %while.112 = (s32[]{:T(128)}, f32[256,8,64]{0,2,1:T(8,128)}, f32[2048,512]{0,1:T(8,128)}, f32[2048,512]{0,1:T(8,128)}, bf16[2048,512]{0,1:T(8,128)(2,1)}, /*inde...) while((s32[]{:T(128)}, f32[256,8,64]{0,2,1:T(8,128)}, ...), condition=%wide.region_41.0_spmd.clone, body=%wide.region_40.0_spmd.clone.sunk | while | flops 680656896 | bytes 33054920 | solution.py:259
  445.1 3.3 constant_dynamic-update-slice_fusion.10
  456.5 3.4 constant_dynamic-update-slice_fusion.10
  473.6 4.0 convert_element_type.659
  484.5 44.3 %while.113 = (s32[]{:T(128)}, f32[256,8,64]{0,2,1:T(8,128)}, f32[2048,512]{0,1:T(8,128)}, f32[2048,512]{0,1:T(8,128)}, bf16[2048,512]{0,1:T(8,128)(2,1)}, /*inde...) while((s32[]{:T(128)}, f32[256,8,64]{0,2,1:T(8,128)}, ...), condition=%wide.region_51.52_spmd.clone, body=%wide.region_50.51_spmd.clone.sunk | while | flops 680656896 | bytes 33054920 | solution.py:259
  490.2 3.4 constant_dynamic-update-slice_fusion.11
  528.8 3.9 convert_element_type.672
  532.7 3.8 convert_element_type.645
  536.6 4.0 convert_element_type.658
  540.7 4.1 convert_element_type.671
  545.4 3.7 multiply_sine_fusion
  554.7 19.4 %reduce-scatter.29.cloned.1.call-done = bf16[256,512]{0,1:T(8,128)(2,1)} async-done(((bf16[2048,512]{0,1:T(8,128)(2,1)}), bf16[256,512]{0,1:T(8,128)(2,1)}) %reduce-scatter.29.cloned.1.call-update) | async-done | bytes 262160 | tf_op jit(solution)/shard_map/reduce_scatter | solution.py:266
  576.6 42.4 %reduce-scatter.19.cloned.1.call-done = bf16[256,512]{0,1:T(8,128)(2,1)} async-done(((bf16[2048,512]{0,1:T(8,128)(2,1)}), bf16[256,512]{0,1:T(8,128)(2,1)}) %reduce-scatter.19.cloned.1.call-update) | async-done | bytes 262160 | tf_op jit(solution)/shard_map/reduce_scatter | solution.py:263
  620.2 43.3 %reduce-scatter.23.cloned.1.call-done = bf16[256,512]{0,1:T(8,128)(2,1)} async-done(((bf16[2048,512]{0,1:T(8,128)(2,1)}), bf16[256,512]{0,1:T(8,128)(2,1)}) %reduce-scatter.23.cloned.1.call-update) | async-done | bytes 262160 | tf_op jit(solution)/shard_map/reduce_scatter | solution.py:263
  664.8 43.5 %reduce-scatter.27.cloned.1.call-done = bf16[256,512]{0,1:T(8,128)(2,1)} async-done(((bf16[2048,512]{0,1:T(8,128)(2,1)}), bf16[256,512]{0,1:T(8,128)(2,1)}) %reduce-scatter.27.cloned.1.call-update) | async-done | bytes 262160 | tf_op jit(solution)/shard_map/reduce_scatter | solution.py:263
  730.5 18.8 %all-reduce.10 = (bf16[2048]{0:T(1024)(128)(2,1)S(1)}, bf16[512]{0:T(512)(128)(2,1)S(1)}, bf16[512]{0:T(512)(128)(2,1)S(1)}, bf16[512]{0:T(512)(128)(2,1)S(1)}, ...) all-reduce(bf16[2048]{0:T(1024)(128)(2,1)S(1)} %add_convert_fusion., ...), channel_id=13, replica_groups=mesh['ctx'=8,'wsh'=4] {'wsh'}, use_global_device_ids=true, to_apply=%region_67.0.clone | all-reduce | flops 5124 | bytes 20496
  751.1 13.0 %all-reduce.8 = (bf16[512]{0:T(512)(128)(2,1)S(1)}, bf16[128]{0:T(256)(128)(2,1)S(1)}, bf16[128]{0:T(256)(128)(2,1)S(1)}, bf16[128]{0:T(256)(128)(2,1)S(1)}, bf1...) all-reduce(bf16[512]{0:T(512)(128)(2,1)S(1)} %dynamic-slice.1, ...), channel_id=1, replica_groups=mesh['ctx'=8,'wsh'=4] {'ctx'}, use_global_device_ids=true, to_apply=%region_68.0 | all-reduce | flops 1281 | bytes 5124 | tf_op jit(solution)/shard_map/psum | solution.py:427
  783.9 14.4 %reduce-scatter.31.cloned.1.call-done = bf16[128,512]{1,0:T(8,128)(2,1)} async-done(((bf16[512,512]{1,0:T(8,128)(2,1)}), bf16[128,512]{1,0:T(8,128)(2,1)}) %reduce-scatter.31.cloned.1.call-update) | async-done | bytes 131088 | tf_op jit(solution)/shard_map/reduce_scatter | solution.py:387
  798.3 44.4 %reduce-scatter.35.cloned.1.call-done = bf16[512,512]{1,0:T(8,128)(2,1)} async-done(((bf16[2048,512]{1,0:T(8,128)(2,1)}), bf16[512,512]{1,0:T(8,128)(2,1)}) %reduce-scatter.35.cloned.1.call-update) | async-done | bytes 524304 | tf_op jit(solution)/shard_map/reduce_scatter | solution.py:396
  842.7 45.4 %reduce-scatter.33.cloned.1.call-done = bf16[512,512]{1,0:T(8,128)(2,1)} async-done(((bf16[512,2048]{1,0:T(8,128)(2,1)}), bf16[512,512]{1,0:T(8,128)(2,1)}) %reduce-scatter.33.cloned.1.call-update) | async-done | bytes 524304 | tf_op jit(solution)/shard_map/reduce_scatter | solution.py:390
  891.2 62.0 %all-reduce.13.cloned.1.call-done = (bf16[512,128]{1,0:T(8,128)(2,1)}, bf16[512,128]{1,0:T(8,128)(2,1)}, bf16[512,128]{1,0:T(8,128)(2,1)}, bf16[128,512]{1,0:T(8...) async-done(((bf16[512,128]{1,0:T(8,128)(2,1)}, bf16[512,128]{1,0:T(8,128)(2,1)}, bf16[512,128]{1,0:T(8,128)(2,1)}, bf16[128,512]{1,0:T(8,128)(2,1)}, ...) | async-done | bytes 1572880 | tf_op jit(solution)/shard_map/psum | solution.py:422
  (806 shorter events, 357.9 us)
Async XLA Ops:
  7.2 148.2 %all-gather.28.cloned.1.call-start = ((), (), s32[]{:S(2)}) async-start(), calls=%async_computation.18 | async-start | bytes 2359296 | tf_op jit(solution)/shard_map/all_gather | solution.py:100
  31.2 128.2 %all-gather.30.cloned.1.call-start = ((), (), s32[]{:S(2)}) async-start(), calls=%async_computation.19 | async-start | bytes 2359296 | tf_op jit(solution)/shard_map/all_gather | solution.py:101
  46.9 153.3 %all-gather.24.cloned.1.call-start = ((), (), s32[]{:S(2)}) async-start(), calls=%async_computation.16 | async-start | bytes 2359296 | tf_op jit(solution)/shard_map/all_gather | solution.py:100
  48.0 156.2 %all-gather.26.cloned.1.call-start = ((), (), s32[]{:S(2)}) async-start(), calls=%async_computation.17 | async-start | bytes 2359296 | tf_op jit(solution)/shard_map/all_gather | solution.py:101
  49.0 193.2 %all-gather.16.cloned.1.call-start = ((), (), s32[]{:S(2)}) async-start(), calls=%async_computation.12 | async-start | bytes 2359296 | tf_op jit(solution)/shard_map/all_gather | solution.py:100
  50.1 196.3 %all-gather.20.cloned.1.call-start = ((), (), s32[]{:S(2)}) async-start(), calls=%async_computation.14 | async-start | bytes 2621440 | tf_op jit(solution)/shard_map/all_gather | solution.py:347
  50.7 222.9 %all-gather.22.cloned.1.call-start = ((), (), s32[]{:S(2)}) async-start(), calls=%async_computation.15 | async-start | bytes 2621440 | tf_op jit(solution)/shard_map/all_gather | solution.py:349
  51.5 251.3 %all-gather.18.cloned.1.call-start = ((), (), s32[]{:S(2)}) async-start(), calls=%async_computation.13 | async-start | bytes 2359296 | tf_op jit(solution)/shard_map/all_gather | solution.py:101
  52.6 499.4 %reduce-scatter.21.cloned.1.call-start = ((), (), s32[]{:S(2)}) async-start(), calls=%async_computation.21 | async-start | bytes 2359296 | tf_op jit(solution)/shard_map/reduce_scatter | solution.py:266
  66.6 48.0 %copy-start.174 = (bf16[128]{0:T(256)(128)(2,1)S(1)}, bf16[128]{0:T(256)(128)(2,1)}, u32[]{:S(2)}) copy-start(bf16[128]{0:T(256)(128)(2,1)} %param.46) | copy-start | bytes 772
  67.6 57.8 %copy-start.175 = (bf16[128]{0:T(256)(128)(2,1)S(1)}, bf16[128]{0:T(256)(128)(2,1)}, u32[]{:S(2)}) copy-start(bf16[128]{0:T(256)(128)(2,1)} %param.49) | copy-start | bytes 772
  67.6 66.2 %copy-start.176 = (bf16[128]{0:T(256)(128)(2,1)S(1)}, bf16[128]{0:T(256)(128)(2,1)}, u32[]{:S(2)}) copy-start(bf16[128]{0:T(256)(128)(2,1)} %param.50) | copy-start | bytes 772
  67.6 74.8 %copy-start.177 = (bf16[128]{0:T(256)(128)(2,1)S(1)}, bf16[128]{0:T(256)(128)(2,1)}, u32[]{:S(2)}) copy-start(bf16[128]{0:T(256)(128)(2,1)} %param.51) | copy-start | bytes 772
  68.6 85.2 %copy-start.136 = (s32[3,256]{1,0:T(4,128)S(1)}, s32[3,256]{1,0:T(4,128)}, u32[]{:S(2)}) copy-start(s32[3,256]{1,0:T(4,128)} %param.37) | copy-start | bytes 9220
  68.6 85.7 %copy-start.161 = (f32[3,256]{1,0:T(4,128)S(1)}, f32[3,256]{1,0:T(4,128)}, u32[]{:S(2)}) copy-start(f32[3,256]{1,0:T(4,128)} %param.36) | copy-start | bytes 9220
  68.6 86.4 %copy-start.42 = (f32[256,512]{1,0:T(8,128)S(1)}, f32[256,512]{1,0:T(8,128)}, u32[]{:S(2)}) copy-start(f32[256,512]{1,0:T(8,128)} %get-tuple-element.1435) | copy-start | bytes 1572868
  85.4 283.3 %copy-start.5 = (bf16[512,512]{1,0:T(8,128)(2,1)}, bf16[512,512]{1,0:T(8,128)(2,1)S(1)}, u32[]{:S(2)}) copy-start(bf16[512,512]{1,0:T(8,128)(2,1)S(1)} %all_gather.43) | copy-start | bytes 1572868
  102.6 241.3 %copy-start.103 = (f32[4,1,128]{2,1,0:T(1,128)}, f32[4,1,128]{2,1,0:T(1,128)S(1)}, u32[]{:S(2)}) copy-start(f32[4,1,128]{2,1,0:T(1,128)S(1)} %convert_element_type.735) | copy-start | bytes 6148
  123.2 157.9 %copy-start.169 = (f32[4,1,128]{2,1,0:T(1,128)}, f32[4,1,128]{2,1,0:T(1,128)S(1)}, u32[]{:S(2)}) copy-start(f32[4,1,128]{2,1,0:T(1,128)S(1)} %convert_element_type.737) | copy-start | bytes 6148
  277.5 88.5 %copy-start.113 = (f32[256]{0:T(256)}, f32[256]{0:T(256)S(1)}, u32[]{:S(2)}) copy-start(f32[256]{0:T(256)S(1)} %broadcast_multiply_fusion.15) | copy-start | bytes 3076
  278.8 87.2 %copy-start.117 = (f32[256]{0:T(256)}, f32[256]{0:T(256)S(1)}, u32[]{:S(2)}) copy-start(f32[256]{0:T(256)S(1)} %add_rsqrt_fusion.3) | copy-start | bytes 3076
  422.3 131.0 %reduce-scatter.25.cloned.1.call-start = ((), (), s32[]{:S(2)}) async-start(), calls=%async_computation.23 | async-start | bytes 2359296 | tf_op jit(solution)/shard_map/reduce_scatter | solution.py:266
  479.2 94.9 %reduce-scatter.29.cloned.1.call-start = ((), (), s32[]{:S(2)}) async-start(), calls=%async_computation.25 | async-start | bytes 2359296 | tf_op jit(solution)/shard_map/reduce_scatter | solution.py:266
  532.7 86.3 %reduce-scatter.19.cloned.1.call-start = ((), (), s32[]{:S(2)}) async-start(), calls=%async_computation.20 | async-start | bytes 2359296 | tf_op jit(solution)/shard_map/reduce_scatter | solution.py:263
  536.6 126.9 %reduce-scatter.23.cloned.1.call-start = ((), (), s32[]{:S(2)}) async-start(), calls=%async_computation.22 | async-start | bytes 2359296 | tf_op jit(solution)/shard_map/reduce_scatter | solution.py:263
  540.6 167.7 %reduce-scatter.27.cloned.1.call-start = ((), (), s32[]{:S(2)}) async-start(), calls=%async_computation.24 | async-start | bytes 2359296 | tf_op jit(solution)/shard_map/reduce_scatter | solution.py:263
  544.8 233.1 %reduce-scatter.37.cloned.1.call-start = ((), (), s32[]{:S(2)}) async-start(), calls=%async_computation.29 | async-start | bytes 655360
  551.7 228.8 %reduce-scatter.41.cloned.1.call-start = ((), (), s32[]{:S(2)}) async-start(), calls=%async_computation.31 | async-start | bytes 655360
  576.5 205.7 %reduce-scatter.39.cloned.1.call-start = ((), (), s32[]{:S(2)}) async-start(), calls=%async_computation.30 | async-start | bytes 655360
  664.8 45.9 %copy-start.49 = (f32[256,512]{1,0:T(8,128)S(1)}, f32[256,512]{1,0:T(8,128)}, u32[]{:S(2)}) copy-start(f32[256,512]{1,0:T(8,128)} %copy-done.48) | copy-start | bytes 1572868
  664.8 45.9 %copy-start.78 = (bf16[256,8,64]{0,2,1:T(8,128)(2,1)S(1)}, bf16[256,8,64]{0,2,1:T(8,128)(2,1)}, u32[]{:S(2)}) copy-start(bf16[256,8,64]{0,2,1:T(8,128)(2,1)} %copy-done.77) | copy-start | bytes 786436
  710.6 87.6 %reduce-scatter.31.cloned.1.call-start = ((), (), s32[]{:S(2)}) async-start(), calls=%async_computation.26 | async-start | bytes 655360 | tf_op jit(solution)/shard_map/reduce_scatter | solution.py:387
  712.9 129.8 %reduce-scatter.35.cloned.1.call-start = ((), (), s32[]{:S(2)}) async-start(), calls=%async_computation.28 | async-start | bytes 2621440 | tf_op jit(solution)/shard_map/reduce_scatter | solution.py:396
  718.9 169.3 %reduce-scatter.33.cloned.1.call-start = ((), (), s32[]{:S(2)}) async-start(), calls=%async_computation.27 | async-start | bytes 2621440 | tf_op jit(solution)/shard_map/reduce_scatter | solution.py:390
  726.7 41.7 %copy-start.158 = (f32[1,256]{1,0:T(1,128)S(1)}, f32[1,256]{1,0:T(1,128)}, u32[]{:S(2)}) copy-start(f32[1,256]{1,0:T(1,128)} %get-tuple-element.1481) | copy-start | bytes 3076
  726.7 41.7 %copy-start.159 = (f32[1,256]{1,0:T(1,128)S(1)}, f32[1,256]{1,0:T(1,128)}, u32[]{:S(2)}) copy-start(f32[1,256]{1,0:T(1,128)} %get-tuple-element.1482) | copy-start | bytes 3076
  726.7 41.7 %copy-start.160 = (f32[1,256]{1,0:T(1,128)S(1)}, f32[1,256]{1,0:T(1,128)}, u32[]{:S(2)}) copy-start(f32[1,256]{1,0:T(1,128)} %get-tuple-element.1483) | copy-start | bytes 3076
  726.7 42.3 %copy-start.155 = (f32[256]{0:T(256)S(1)}, f32[256]{0:T(256)}, u32[]{:S(2)}) copy-start(f32[256]{0:T(256)} %get-tuple-element.1511) | copy-start | bytes 3076
  726.7 42.3 %copy-start.156 = (f32[256]{0:T(256)S(1)}, f32[256]{0:T(256)}, u32[]{:S(2)}) copy-start(f32[256]{0:T(256)} %get-tuple-element.1557) | copy-start | bytes 3076
  726.7 42.3 %copy-start.157 = (f32[256]{0:T(256)S(1)}, f32[256]{0:T(256)}, u32[]{:S(2)}) copy-start(f32[256]{0:T(256)} %get-tuple-element.1501) | copy-start | bytes 3076
  726.8 226.4 %all-reduce.13.cloned.1.call-start = ((), (), s32[]{:S(2)}) async-start(), calls=%async_computation.32 | async-start | bytes 3145728 | tf_op jit(solution)/shard_map/psum | solution.py:422
  729.6 44.2 %copy-start.28 = (bf16[3,256,512]{2,1,0:T(8,128)(2,1)S(1)}, bf16[3,256,512]{2,1,0:T(8,128)(2,1)}, u32[]{:S(2)}) copy-start(bf16[3,256,512]{2,1,0:T(8,128)(2,1)} %param.54) | copy-start | bytes 2359300
  729.6 44.2 %copy-start.122 = (f32[256]{0:T(256)S(1)}, f32[256]{0:T(256)}, u32[]{:S(2)}) copy-start(f32[256]{0:T(256)} %copy-done.121) | copy-start | bytes 3076
  729.6 44.2 %copy-start.124 = (f32[256]{0:T(256)S(1)}, f32[256]{0:T(256)}, u32[]{:S(2)}) copy-start(f32[256]{0:T(256)} %copy-done.123) | copy-start | bytes 3076
  729.6 44.2 %copy-start.126 = (f32[256]{0:T(256)S(1)}, f32[256]{0:T(256)}, u32[]{:S(2)}) copy-start(f32[256]{0:T(256)} %copy-done.125) | copy-start | bytes 3076
  780.1 108.1 %copy-start.15 = (bf16[512,512]{1,0:T(8,128)(2,1)S(1)}, bf16[512,512]{1,0:T(8,128)(2,1)}, u32[]{:S(2)}) copy-start(bf16[512,512]{1,0:T(8,128)(2,1)} %copy-done.14) | copy-start | bytes 1572868
  780.5 107.7 %copy-start.94 = (bf16[256,512]{0,1:T(8,128)(2,1)S(1)}, bf16[256,512]{0,1:T(8,128)(2,1)}, u32[]{:S(2)}) copy-start(bf16[256,512]{0,1:T(8,128)(2,1)} %reduce-scatter.21.cloned.1.call-done) | copy-start | bytes 786436
  780.5 108.1 %copy-start.92 = (bf16[256,512]{0,1:T(8,128)(2,1)S(1)}, bf16[256,512]{0,1:T(8,128)(2,1)}, u32[]{:S(2)}) copy-start(bf16[256,512]{0,1:T(8,128)(2,1)} %reduce-scatter.25.cloned.1.call-done) | copy-start | bytes 786436
  (164 other events, 939.7 us)
Sparse Core Ops, SparseCore 0:
  31.3 27.9 all-gather.27
  61.2 27.8 all-gather.29
  91.6 27.8 all-gather.23
  121.8 27.8 all-gather.25
  152.1 27.8 all-gather.15
  181.4 45.9 all-gather.19
  229.0 44.6 all-gather.21
  276.1 26.5 all-gather.17
  422.4 41.2 reduce-scatter.20
  479.4 41.0 reduce-scatter.24
  532.8 41.3 reduce-scatter.28
  577.6 41.2 reduce-scatter.18
  622.2 41.2 reduce-scatter.22
  667.0 41.2 reduce-scatter.26
  710.4 21.6 reduce-scatter.36
  734.2 19.9 reduce-scatter.40
  756.3 19.8 reduce-scatter.38
  778.4 19.8 reduce-scatter.30
  800.6 42.1 reduce-scatter.34
  845.0 43.1 reduce-scatter.32
  893.3 59.8 all-reduce.12
where the time goes:
time: 979 us; the launch traced here: 969 us
  waiting for transfers between devices  360 us (37%)
  matrix products  175 us (18%)
  blocking collectives  156 us (16%)
  other arithmetic  142 us (15%)
  local copies, waits for them, and re-layouts  110 us (11%)
  between operations  22.8 us (2%)
    reduce_scatter x3, waiting for transfers between devices, run_batch(): lax.psum_scatter(grad_keys.astype(jnp.bfloat16), 'ctx', scatter_dimension...  129 us
    psum x1, waiting for transfers between devices, body(): lax.psum(shares[0].astype(jnp.bfloat16), 'ctx').astype(jnp.float32)  62 us
    unnamed x380, local copies, waits for them, and re-layouts  46.1 us
    reduce_scatter x1, waiting for transfers between devices, body(): lax.psum_scatter(summed[4].astype(jnp.bfloat16), 'wsh', scatter_dimension...  45.4 us
    reduce_scatter x1, waiting for transfers between devices, body(): lax.psum_scatter(summed[6].astype(jnp.bfloat16), 'wsh', scatter_dimension...  44.4 us
    dynamic_update_slice x12, other arithmetic, revisit_sweep(): lax.dynamic_update_slice_in_dim(grad_values, lax.dynamic_slice_in_dim(gra...  39.2 us
    reduce_sum x12, other arithmetic, attend_sweep(): row_mass = row_mass * factor + jnp.sum(exponent, axis=2)  36.5 us
    dot_general x12, matrix products, attend_sweep(): jnp.einsum('qhd,khd->hqk', query_heads, key_part, preferred_element_type=...  33 us
  transfers between devices with their start and end apart: 21, of which 10 were waited for; matrix products, arithmetic and copies ran while one was open for 29% of the time, Pallas kernels for 0%

commit v1 on v0

v1 whole, which is shorter than its diff:
```python
import functools
import math

import jax
import jax.numpy as jnp
from jax import lax
from jax.experimental import pallas as pl
from jax.experimental.pallas import tpu as pltpu
from jax.sharding import PartitionSpec as P

HEADS = 8
PAIRS = 4
WIDE = 128
SMALL = 16
epsilon = 1e-06
f32 = jnp.float32
bf16 = jnp.bfloat16
LOG2E = math.log2(math.e)
NT = (((1,), (1,)), ((), ()))
TN = (((0,), (0,)), ((), ()))
NN = (((1,), (0,)), ((), ()))
MIB = 1024 * 1024


def room(mebibytes):
    return pltpu.CompilerParams(vmem_limit_bytes=int(mebibytes) * MIB)


def cost(micros):
    return pl.CostEstimate(flops=int(micros * 1.1e9), bytes_accessed=1024, transcendentals=0)


def dot(a, b, dims=NN):
    return lax.dot_general(a, b, dims, preferred_element_type=f32)


def lane_masks(shape):
    lane = lax.broadcasted_iota(jnp.int32, shape, 1)
    return lane < WIDE // 2


def attend_kernel(blocks, carried, q_ref, *refs):
    kv_refs = refs[:blocks]
    refs = refs[blocks + carried :]
    o_ref, mass_ref, low_refs = refs[0], refs[1], refs[2:]
    scale = 0.125 * LOG2E
    q = q_ref[0]
    first = lane_masks(q.shape)
    none = jnp.zeros_like(q)
    outs, masses = [], []
    for head in range(2):
        mine = jnp.where(first, q, none) if head == 0 else jnp.where(first, none, q)
        chunks = []
        for ref in kv_refs:
            for start in range(0, ref.shape[1], 512):
                chunks.append((ref, start))
        scores = [dot(mine, ref[0, start : start + 512, :WIDE], NT) for ref, start in chunks]
        top = functools.reduce(jnp.maximum, scores)
        top = jnp.max(top, axis=1, keepdims=True)
        lift = top * scale
        total = None
        weighted = None
        for piece, (ref, start) in zip(scores, chunks):
            e = jnp.exp2(piece * scale - lift)
            part = sum(e[:, i : i + 128] for i in range(0, 512, 128))
            total = part if total is None else total + part
            w = dot(e.astype(bf16), ref[0, start : start + 512, WIDE:])
            weighted = w if weighted is None else weighted + w
        total = jnp.sum(total, axis=1, keepdims=True)
        outs.append(weighted * (1.0 / total))
        masses.append(lift + jnp.log2(total))
    out = jnp.where(first, outs[0], outs[1])
    o_ref[0] = out
    low = out.astype(bf16)
    for d, ref in enumerate(low_refs):

        @pl.when(pl.program_id(0) == d)
        def _(ref=ref):
            ref[0] = low

    table = jnp.where(first, masses[0], masses[1])
    turned = jnp.transpose(table)
    mass_ref[0] = jnp.concatenate([turned[0:4], turned[64:68]], axis=0)


def attend(at, seqs, q, kvs, before):
    _, rows, _ = q.shape
    step = rows // PAIRS
    keys = sum(kv.shape[1] for kv in kvs)
    shapes = [
        jax.ShapeDtypeStruct((seqs, rows, WIDE), f32),
        jax.ShapeDtypeStruct((seqs, 8, rows), f32),
    ] + [jax.ShapeDtypeStruct((seqs, step, WIDE), bf16)] * PAIRS
    carried = len(shapes) if before else 0
    return pl.pallas_call(
        functools.partial(attend_kernel, len(kvs), carried),
        grid=(PAIRS,),
        in_specs=[pl.BlockSpec((1, step, WIDE), lambda i: (0, i, 0))]
        + [full_spec(kv) for kv in kvs]
        + [pl.BlockSpec(memory_space=pl.ANY)] * carried,
        out_specs=[
            pl.BlockSpec((1, step, WIDE), lambda i: (at, i, 0)),
            pl.BlockSpec((1, 8, step), lambda i: (at, 0, i)),
        ]
        + [pl.BlockSpec((1, step, WIDE), lambda i: (at, 0, 0))] * PAIRS,
        out_shape=shapes,
        input_output_aliases={1 + len(kvs) + i: i for i in range(carried)},
        compiler_params=room(10 + keys // 256),
        cost_estimate=cost(4),
        name="attend",
    )(q, *kvs, *(before or ()))


def attend_back_kernel(blocks, q_ref, *refs):
    g_refs, o_ref, mass_ref = refs[:PAIRS], refs[PAIRS], refs[PAIRS + 1]
    refs = refs[PAIRS + 2 :]
    kv_refs = refs[:blocks]
    dq_ref = refs[blocks]
    dkv_refs = refs[blocks + 1 : 2 * blocks + 1]
    dq_acc = refs[2 * blocks + 1]
    scale = 0.125 * LOG2E
    q = q_ref[0]
    g = jnp.concatenate([ref[0] for ref in g_refs], axis=0)
    first = lane_masks(q.shape)
    none = jnp.zeros_like(q)
    qs = [jnp.where(first, q, none), jnp.where(first, none, q)]
    gs = [jnp.where(first, g, none), jnp.where(first, none, g)]
    product = g.astype(f32) * o_ref[0]
    which = lax.broadcasted_iota(jnp.int32, (8, WIDE), 0) == (
        lax.broadcasted_iota(jnp.int32, (8, WIDE), 1) // (WIDE // 2)
    )
    deltas = lax.dot_general(
        which.astype(f32), product, NT, precision=lax.Precision.HIGHEST, preferred_element_type=f32
    )
    delta = [deltas[0:1], deltas[1:2]]
    mass = [mass_ref[0, 0:1, :], mass_ref[0, 4:5, :]]
    dq_acc[...] = jnp.zeros_like(dq_acc)
    size = 256
    key_first = lane_masks((size, WIDE))
    key_none = jnp.zeros((size, WIDE), bf16)

    for kv_ref, dkv_ref in zip(kv_refs, dkv_refs):

        def chunk(i, carry, kv_ref=kv_ref, dkv_ref=dkv_ref):
            at = pl.ds(pl.multiple_of(i * size, size), size)
            k = kv_ref[0, at, :WIDE]
            v = kv_ref[0, at, WIDE:]
            dk = dv = dq = None
            for head in range(2):
                s = dot(k, qs[head], NT)
                p = jnp.exp2(s * scale - mass[head])
                dp = dot(v, gs[head], NT)
                ds = (p * (dp - delta[head])).astype(bf16)
                own_v = dot(p.astype(bf16), gs[head])
                own_k = dot(ds, qs[head])
                km = jnp.where(key_first, k, key_none) if head == 0 else jnp.where(key_first, key_none, k)
                own_q = dot(ds, km, TN)
                dv = own_v if dv is None else dv + own_v
                dk = own_k if dk is None else dk + own_k
                dq = own_q if dq is None else dq + own_q
            dkv_ref[0, at, :WIDE] = (dk * 0.125).astype(dkv_ref.dtype)
            dkv_ref[0, at, WIDE:] = dv.astype(dkv_ref.dtype)
            dq_acc[...] += dq
            return carry

        lax.fori_loop(0, kv_ref.shape[1] // size, chunk, 0)
    dq_ref[0] = (dq_acc[...] * 0.125).astype(bf16)


def attend_back(at, q, gs, o, mass, kvs, kinds):
    _, rows, _ = q.shape
    keys = sum(kv.shape[1] for kv in kvs)
    own = gs[0].shape[1]
    whole = lambda width: pl.BlockSpec((1, rows, width), lambda s: (0, 0, 0))
    kv_specs = [pl.BlockSpec((1, kv.shape[1], 2 * WIDE), lambda s: (0, 0, 0)) for kv in kvs]
    return pl.pallas_call(
        functools.partial(attend_back_kernel, len(kvs)),
        grid=(1,),
        in_specs=[whole(WIDE)]
        + [pl.BlockSpec((1, own, WIDE), lambda s: (at, 0, 0))] * PAIRS
        + [pl.BlockSpec((1, rows, WIDE), lambda s: (at, 0, 0)), pl.BlockSpec((1, 8, rows), lambda s: (at, 0, 0))]
        + kv_specs,
        out_specs=[whole(WIDE)] + kv_specs,
        out_shape=[jax.ShapeDtypeStruct((1, rows, WIDE), bf16)]
        + [jax.ShapeDtypeStruct(kv.shape, kind) for kv, kind in zip(kvs, kinds)],
        scratch_shapes=[pltpu.VMEM((rows, WIDE), f32)],
        compiler_params=room(14 + keys // 512),
        cost_estimate=cost(14),
        name="attend_back",
    )(q, *gs, o, mass, *kvs)


def full_spec(array):
    return pl.BlockSpec(array.shape, lambda *_: (0,) * array.ndim)


def pack_kernel(info_ref, *refs):
    parts, out_ref = refs[:-1], refs[-1]
    core = info_ref[0]
    half = out_ref.shape[0]

    @pl.when(core == 0)
    def _():
        out_ref[...] = jnp.concatenate([ref[:half] for ref in parts], axis=1)

    @pl.when(core != 0)
    def _():
        out_ref[...] = jnp.concatenate([ref[half:] for ref in parts], axis=1)


def pack(info, parts):
    rows, width = parts[0].shape
    shape = (rows // 2, len(parts) * width)
    return pl.pallas_call(
        pack_kernel,
        grid=(1,),
        in_specs=[pl.BlockSpec(memory_space=pltpu.SMEM)] + [full_spec(x) for x in parts],
        out_specs=pl.BlockSpec(shape, lambda i: (0, 0)),
        out_shape=jax.ShapeDtypeStruct(shape, bf16),
        compiler_params=room(6),
        cost_estimate=cost(1),
        name="pack",
    )(info, *parts)


def pack_feed_kernel(info_ref, inner_ref, outer_ref, wout_ref, bias_ref, *refs):
    vectors, out_ref = refs[:-1], refs[-1]
    core = info_ref[0]
    width = inner_ref.shape[0]
    cut = wout_ref.shape[0] // 2

    @pl.when(core == 0)
    def _():
        out_ref[:width] = inner_ref[...]
        out_ref[width : width + cut] = wout_ref[:cut]

    @pl.when(core != 0)
    def _():
        out_ref[:width] = outer_ref[...]
        out_ref[width : width + cut] = wout_ref[cut:]

    row = lax.broadcasted_iota(jnp.int32, (SMALL, WIDE), 0)
    table = jnp.zeros((SMALL, WIDE), f32)
    for i, ref in enumerate(vectors):
        table = jnp.where(row == i + 1, ref[...].astype(f32), table)
    row = lax.broadcasted_iota(jnp.int32, (SMALL, width), 0)
    table = jnp.concatenate([table, jnp.zeros((SMALL, width - WIDE), f32)], axis=1)
    table = jnp.where(row == 0, bias_ref[...].astype(f32), table)
    out_ref[width + cut :] = table.astype(bf16)


def pack_feed(info, w_inner, w_outer, w_out, b_inner, vectors):
    width = w_inner.shape[0]
    parts = [w_inner, w_outer, w_out, b_inner.reshape(1, -1)] + [v.reshape(1, -1) for v in vectors]
    shape = (width + w_out.shape[0] // 2 + SMALL, w_out.shape[1])
    return pl.pallas_call(
        pack_feed_kernel,
        grid=(1,),
        in_specs=[pl.BlockSpec(memory_space=pltpu.SMEM)] + [full_spec(x) for x in parts],
        out_specs=pl.BlockSpec(shape, lambda i: (0, 0)),
        out_shape=jax.ShapeDtypeStruct(shape, bf16),
        compiler_params=room(10),
        cost_estimate=cost(2),
        name="pack_feed",
    )(info, *parts)


def project_kernel(count, *refs):
    blocks, w_ref, q_ref, kv_ref = refs[:count], refs[count], refs[count + 1], refs[count + 2]
    at = 0
    for ref in blocks:
        rows = ref.shape[1]
        made = dot(ref[0], w_ref[0]).astype(bf16)
        q_ref[0, at : at + rows] = made[:, :WIDE]
        kv_ref[0, at : at + rows] = made[:, WIDE:]
        at += rows


def project(at, tokens, w_order):
    total = sum(x.shape[1] for x in tokens)
    return pl.pallas_call(
        functools.partial(project_kernel, len(tokens)),
        grid=(1,),
        in_specs=[pl.BlockSpec((1,) + x.shape[1:], lambda i: (at, 0, 0)) for x in tokens]
        + [pl.BlockSpec((1,) + w_order.shape[1:], lambda i: (0, 0, 0))],
        out_specs=[
            pl.BlockSpec((1, total, WIDE), lambda i: (0, 0, 0)),
            pl.BlockSpec((1, total, 2 * WIDE), lambda i: (0, 0, 0)),
        ],
        out_shape=[
            jax.ShapeDtypeStruct((1, total, WIDE), bf16),
            jax.ShapeDtypeStruct((1, total, 2 * WIDE), bf16),
        ],
        compiler_params=room(10),
        cost_estimate=cost(1),
        name="project",
    )(*tokens, w_order)


def combine_kernel(chosen, count, prior, final, info_ref, *refs):
    blocks, refs = refs[:count], refs[count:]
    backs, refs = refs[: 3 * len(chosen)], refs[3 * len(chosen) :]
    grad = None
    if prior:
        grad, refs = refs[0][...], refs[1:]
    outs, grad_refs = refs[:PAIRS], refs[PAIRS:]
    rows = outs[0].shape[1]
    for i, s in enumerate(chosen):
        dq_ref, kept_ref, got_ref = backs[3 * i : 3 * i + 3]
        at = 0
        for ref in blocks:
            size = ref.shape[1]
            part = slice(at, at + size)
            dkv = (kept_ref[0, part] + got_ref[0, part].astype(f32)).astype(bf16)
            piece = jnp.concatenate([dq_ref[0, part], dkv], axis=1)
            outs[at // rows][i, at % rows : at % rows + size] = piece
            term = dot(ref[s], piece, TN)
            grad = term if grad is None else grad + term
            at += size
    if not final:
        grad_refs[0][...] = grad
        return
    size = grad.shape[0] // (2 * PAIRS)

    def write(even_ref, odd_ref):
        for c in range(2 * PAIRS):
            ref = even_ref if c % 2 == 0 else odd_ref
            ref[jnp.bitwise_xor(c // 2, info_ref[2])] = grad[c * size : (c + 1) * size].astype(ref.dtype)

    @pl.when(info_ref[0] == 0)
    def _():
        write(grad_refs[0], grad_refs[1])

    @pl.when(info_ref[0] != 0)
    def _():
        write(grad_refs[1], grad_refs[0])


def combine(info, chosen, tokens, backs, prior, final):
    _, rows, width = tokens[0].shape
    flat = [x for back in backs for x in back]
    extra = [] if prior is None else [prior]
    if final:
        shape = (PAIRS, width // (2 * PAIRS), 3 * WIDE)
        grads = [jax.ShapeDtypeStruct(shape, f32), jax.ShapeDtypeStruct(shape, bf16)]
    else:
        grads = [jax.ShapeDtypeStruct((width, 3 * WIDE), f32)]
    pieces = [jax.ShapeDtypeStruct((len(chosen), rows, 3 * WIDE), bf16)] * PAIRS
    return pl.pallas_call(
        functools.partial(combine_kernel, chosen, len(tokens), len(extra), final),
        grid=(1,),
        in_specs=[pl.BlockSpec(memory_space=pltpu.SMEM)] + [full_spec(x) for x in tokens + flat + extra],
        out_specs=[full_spec(x) for x in pieces + grads],
        out_shape=pieces + grads,
        compiler_params=room(20),
        cost_estimate=cost(2),
        name="combine",
    )(info, *tokens, *flat, *extra)


def join_small_kernel(keep_ref, got_ref, *outs):
    for d, out in enumerate(outs):
        out[...] = (keep_ref[d] + got_ref[d].astype(f32)).astype(bf16)


def join_small(keep, got):
    return pl.pallas_call(
        join_small_kernel,
        grid=(1,),
        in_specs=[full_spec(keep), full_spec(got)],
        out_specs=[pl.BlockSpec(keep.shape[1:], lambda i: (0, 0))] * PAIRS,
        out_shape=[jax.ShapeDtypeStruct(keep.shape[1:], bf16)] * PAIRS,
        compiler_params=room(6),
        cost_estimate=cost(1),
        name="join_small",
    )(keep, got)


def share_small_kernel(info_ref, *refs):
    parts, outs = refs[:PAIRS], refs[PAIRS:]
    for step, out in enumerate(outs):
        at = jnp.bitwise_xor(jnp.bitwise_xor(info_ref[1], info_ref[2]), step)
        value = parts[0][...]
        for d in range(1, PAIRS):
            value = jnp.where(at == d, parts[d][...], value)
        out[...] = value


def share_small(info, parts):
    return pl.pallas_call(
        share_small_kernel,
        grid=(1,),
        in_specs=[pl.BlockSpec(memory_space=pltpu.SMEM)] + [full_spec(x) for x in parts],
        out_specs=[full_spec(x) for x in parts],
        out_shape=[jax.ShapeDtypeStruct(x.shape, bf16) for x in parts],
        compiler_params=room(6),
        cost_estimate=cost(1),
        name="share_small",
    )(info, *parts)


def state_kernel(base_ref, *refs):
    blocks, w_ref, out_ref = refs[:PAIRS], refs[PAIRS], refs[PAIRS + 1]
    total = base_ref[0]
    for d, ref in enumerate(blocks):
        total = total + dot(ref[0], w_ref[d], NT)
    out_ref[0] = total


def add_state(at, place, base, blocks, w_order):
    rows, width = base.shape[1:]
    return pl.pallas_call(
        state_kernel,
        grid=(1,),
        in_specs=[pl.BlockSpec((1, rows, width), lambda i: (at, 0, 0))]
        + [pl.BlockSpec((1,) + b.shape[1:], lambda i: (place, 0, 0)) for b in blocks]
        + [full_spec(w_order)],
        out_specs=pl.BlockSpec((1, rows, width), lambda i: (at, 0, 0)),
        out_shape=jax.ShapeDtypeStruct(base.shape, base.dtype),
        input_output_aliases={0: 0},
        compiler_params=room(10),
        cost_estimate=cost(2.5),
        name="add_state",
    )(base, *blocks, w_order)


def assemble_kernel(info_ref, *refs):
    mine, other, out_ref = refs[:PAIRS], refs[PAIRS : 2 * PAIRS], refs[2 * PAIRS]
    core, zed, pair = info_ref[0], info_ref[1], info_ref[2]
    half = mine[0].shape[0]
    for a in range(PAIRS):
        order = jnp.bitwise_xor(lax.rem(zed + a, PAIRS), pair)
        for side in range(2):
            step = (-a) % PAIRS if side == 0 else a
            piece = jnp.where(core == side, mine[step][...], other[step][...])
            out_ref[order, side * half : (side + 1) * half] = piece


def assemble(info, mine, other):
    half, width = mine[0].shape
    shape = (PAIRS, 2 * half, width)
    return pl.pallas_call(
        assemble_kernel,
        grid=(1,),
        in_specs=[pl.BlockSpec(memory_space=pltpu.SMEM)] + [full_spec(x) for x in mine + other],
        out_specs=pl.BlockSpec(shape, lambda i: (0, 0, 0)),
        out_shape=jax.ShapeDtypeStruct(shape, bf16),
        compiler_params=room(10),
        cost_estimate=cost(3),
        name="assemble",
    )(info, *mine, *other)


def keep_scalar(block):
    tail = block[-8:]
    total = tail[:, :WIDE] + tail[:, WIDE : 2 * WIDE]
    high = total.astype(bf16).astype(f32)
    split = jnp.concatenate([high, total - high, tail[:, 2 * WIDE :]], axis=1)
    row = lax.broadcasted_iota(jnp.int32, tail.shape, 0)
    tail = jnp.where(row == 6, split, tail)
    return tail if block.shape[0] == 8 else jnp.concatenate([block[:-8], tail], axis=0)


def flat_rows(ref):
    return ref[...].reshape(-1, ref.shape[-1])


def write_pieces(info_ref, even_ref, odd_ref, grads, small):
    pieces = 2 * PAIRS * even_ref.shape[1]

    def write(keep_ref, give_ref):
        for c in range(pieces):
            ref = keep_ref if c % 2 == 0 else give_ref
            order = jnp.bitwise_xor((c // 2) % PAIRS, info_ref[2])
            repeat = c // (2 * PAIRS)
            at = 0
            for grad in grads:
                size = grad.shape[0] // pieces
                ref[order, repeat, 0, at : at + size] = grad[c * size : (c + 1) * size]
                at += size
            if small is not None:
                ref[order, repeat, 0, at : at + 8] = small if c == 0 else jnp.zeros_like(small)

    @pl.when(info_ref[0] == 0)
    def _():
        write(even_ref, odd_ref)

    @pl.when(info_ref[0] != 0)
    def _():
        write(odd_ref, even_ref)


def outer_grad_kernel(
    info_ref, a0_ref, a1_ref, a2_ref, a3_ref, ilow_ref, gfeed_ref, gbranch_ref, even_ref, odd_ref
):
    g_outer = dot(flat_rows(ilow_ref), flat_rows(gfeed_ref), TN).astype(bf16)
    order = jnp.bitwise_xor(pl.program_id(0), info_ref[2])
    low, high = order % 2 == 0, order < 2
    att = jnp.where(
        high,
        jnp.where(low, flat_rows(a0_ref), flat_rows(a1_ref)),
        jnp.where(low, flat_rows(a2_ref), flat_rows(a3_ref)),
    )
    g_out = dot(att, flat_rows(gbranch_ref), TN).astype(bf16)
    write_pieces(info_ref, even_ref, odd_ref, (g_outer, g_out), None)


def inner_grad_kernel(info_ref, nlow_ref, gin_ref, vsum_ref, bsum_ref, even_ref, odd_ref):
    g_in = dot(flat_rows(nlow_ref), flat_rows(gin_ref), TN).astype(bf16)
    vectors = sum(vsum_ref[s] for s in range(vsum_ref.shape[0]))
    bias = sum(bsum_ref[s] for s in range(bsum_ref.shape[0]))
    width = g_in.shape[1]
    low = jnp.concatenate([vectors, jnp.zeros((8, width - WIDE), f32)], axis=1)
    row = lax.broadcasted_iota(jnp.int32, (8, width), 0)
    small = keep_scalar(jnp.where(row == 7, bias, low)).astype(bf16)
    write_pieces(info_ref, even_ref, odd_ref, (g_in,), small)


def split_grads(kernel, name, info, arrays, specs, piece, width, ctx):
    shape = (PAIRS, ctx // (2 * PAIRS), PAIRS, piece, width)
    out_spec = pl.BlockSpec(shape[:2] + (1, piece, width), lambda z, info: (0, 0, z, 0, 0))
    return pl.pallas_call(
        kernel,
        grid_spec=pltpu.PrefetchScalarGridSpec(
            num_scalar_prefetch=1, grid=(PAIRS,), in_specs=specs, out_specs=[out_spec, out_spec]
        ),
        out_shape=[jax.ShapeDtypeStruct(shape, bf16)] * 2,
        compiler_params=room(24),
        cost_estimate=cost(4.5),
        name=name,
    )(info, *arrays)


def hidden_spec(array):
    seqs, rows, hidden = array.shape
    return pl.BlockSpec(
        (seqs, rows, hidden // PAIRS), lambda z, info: (0, 0, lax.rem(z - info[1] + PAIRS, PAIRS))
    )


def outer_grads(info, att, ilow, gfeed, gbranch, ctx):
    width = gfeed.shape[2]
    piece = (ilow.shape[2] // PAIRS + width // PAIRS) // ctx
    arrays = [*att, ilow, gfeed, gbranch]
    specs = [full_spec(x) for x in arrays]
    specs[PAIRS] = hidden_spec(ilow)
    return split_grads(outer_grad_kernel, "outer_grads", info, arrays, specs, piece, width, ctx)


def inner_grads(info, nlow, gin, vsum, bsum, ctx):
    width = nlow.shape[2]
    seqs = vsum.shape[0]
    specs = [
        full_spec(nlow),
        hidden_spec(gin),
        pl.BlockSpec((seqs, 8, WIDE), lambda z, info: (0, 0, z)),
        hidden_spec(bsum),
    ]
    piece = width // ctx + 8
    return split_grads(
        inner_grad_kernel, "inner_grads", info, [nlow, gin, vsum, bsum], specs, piece, gin.shape[2] // PAIRS, ctx
    )


def join_kernel(scalar, keep_ref, got_ref, *outs):
    for d, out in enumerate(outs):
        for r in range(out.shape[0]):
            total = keep_ref[d, r, 0].astype(f32) + got_ref[d, r, 0].astype(f32)
            out[r, 0] = (keep_scalar(total) if scalar else total).astype(bf16)


def join(keep, got, scalar):
    _, repeats, wsh, piece, width = keep.shape
    spec = pl.BlockSpec((PAIRS, repeats, 1, piece, width), lambda z: (0, 0, z, 0, 0))
    return pl.pallas_call(
        functools.partial(join_kernel, scalar),
        grid=(wsh,),
        in_specs=[spec, spec],
        out_specs=[pl.BlockSpec((repeats, 1, piece, width), lambda z: (0, z, 0, 0))] * PAIRS,
        out_shape=[jax.ShapeDtypeStruct(keep.shape[1:], bf16)] * PAIRS,
        compiler_params=room(16),
        cost_estimate=cost(1.5),
        name="join",
    )(keep, got)


def share_kernel(info_ref, *refs):
    firsts, seconds, outs = refs[:PAIRS], refs[PAIRS : 2 * PAIRS], refs[2 * PAIRS :]
    for step in range(PAIRS):
        place = jnp.bitwise_xor(info_ref[1], step)
        out = outs[step % 2]
        for r in range(out.shape[0]):
            totals = []
            for parts in (firsts, seconds):
                total = parts[0][r, place].astype(f32)
                for part in parts[1:]:
                    total = total + part[r, place].astype(f32)
                totals.append(total)
            size = totals[0].shape[0]
            out[r, step // 2, :size] = totals[0].astype(bf16)
            out[r, step // 2, size:] = keep_scalar(totals[1]).astype(bf16)


def share_parts(info, firsts, seconds):
    repeats, wsh, piece, width = firsts[0].shape
    shape = (repeats, wsh // 2, piece + seconds[0].shape[2], width)
    return pl.pallas_call(
        share_kernel,
        grid=(1,),
        in_specs=[pl.BlockSpec(memory_space=pltpu.SMEM)] + [full_spec(x) for x in firsts + seconds],
        out_specs=[pl.BlockSpec(shape, lambda i: (0, 0, 0, 0))] * 2,
        out_shape=[jax.ShapeDtypeStruct(shape, bf16)] * 2,
        compiler_params=room(16),
        cost_estimate=cost(1.5),
        name="share",
    )(info, *firsts, *seconds)


def halve_kernel(keep_ref, got_ref, own_ref, send_ref):
    for at, out in enumerate((own_ref, send_ref)):
        out[...] = keep_scalar(keep_ref[at].astype(f32) + got_ref[at].astype(f32)).astype(bf16)


def halve(keep, got):
    shape = keep.shape[1:]
    return pl.pallas_call(
        halve_kernel,
        grid=(1,),
        in_specs=[full_spec(keep), full_spec(got)],
        out_specs=[pl.BlockSpec(shape, lambda i: (0, 0))] * 2,
        out_shape=[jax.ShapeDtypeStruct(shape, bf16)] * 2,
        compiler_params=room(6),
        cost_estimate=cost(1),
        name="halve",
    )(keep, got)


def total_kernel(count, *refs):
    feeds, heads, out = refs[:count], refs[count:-1], refs[-1]
    total = feeds[0][...].astype(f32)
    for part in feeds[1:]:
        total = total + part[...].astype(f32)
    out[: total.shape[0]] = keep_scalar(total).astype(bf16)
    if heads:
        at = total.shape[0]
        total = heads[0][...].astype(f32)
        for part in heads[1:]:
            total = total + part[...].astype(f32)
        rows = total.shape[0]
        kept = rows * 3 // 4
        rest = [total[kept:, i * WIDE : (i + 1) * WIDE] for i in range(3)]
        out[at:] = jnp.concatenate([total[:kept], jnp.concatenate(rest, axis=0)], axis=1).astype(bf16)


def total_parts(feeds, heads):
    rows, width = feeds[0].shape
    extra = heads[0].shape[0] * 3 // 4 if heads else 0
    shape = (rows + extra, width)
    return pl.pallas_call(
        functools.partial(total_kernel, len(feeds)),
        grid=(1,),
        in_specs=[full_spec(x) for x in feeds + heads],
        out_specs=pl.BlockSpec(shape, lambda i: (0, 0)),
        out_shape=jax.ShapeDtypeStruct(shape, bf16),
        compiler_params=room(6),
        cost_estimate=cost(1),
        name="total",
    )(*feeds, *heads)


def unpack_kernel(info_ref, *refs):
    pieces = refs[: 2 * PAIRS]
    outer_ref, out_ref, in_ref, tail_ref, *heads = refs[2 * PAIRS :]
    core, pair = info_ref[0], info_ref[2]
    for side in range(2):
        for d in range(PAIRS):
            ref = pieces[side * PAIRS + d]
            place = jnp.bitwise_xor(pair, d) * 2 + jnp.bitwise_xor(core, side)
            at = 0
            for target in (outer_ref, out_ref, in_ref):
                size = target.shape[0] // (2 * PAIRS)
                start = pl.multiple_of(place * size, size)
                target[pl.ds(start, size)] = ref[at : at + size].astype(f32)
                at += size

            @pl.when(place == 0)
            def _(ref=ref, at=at):
                tail_ref[...] = ref[at : at + 8].astype(f32)

            at += 8
            size = heads[0].shape[0] // (2 * PAIRS)
            kept = size * 3 // 4
            for i, target in enumerate(heads):
                start = pl.multiple_of(place * size, size)
                target[pl.ds(start, kept)] = ref[at : at + kept, i * WIDE : (i + 1) * WIDE].astype(f32)
                more = (size - kept) * i + at
                target[pl.ds(start + kept, size - kept)] = ref[more : more + size - kept, 3 * WIDE :].astype(f32)


def unpack(info, mine, other, part, out_rows):
    width = mine[0].shape[1]
    shapes = [(part, width), (out_rows, width), (width, part), (8, width)] + [(width, WIDE)] * 3
    return pl.pallas_call(
        unpack_kernel,
        grid=(1,),
        in_specs=[pl.BlockSpec(memory_space=pltpu.SMEM)] + [full_spec(x) for x in mine + other],
        out_specs=[pl.BlockSpec(shape, lambda i: (0, 0)) for shape in shapes],
        out_shape=[jax.ShapeDtypeStruct(shape, f32) for shape in shapes],
        compiler_params=room(16),
        cost_estimate=cost(3),
        name="unpack",
    )(info, *mine, *other)


def gelu_parts(x):
    half = 0.5 * (1.0 + lax.erf(x * 2.0 ** (-0.5)))
    density = jnp.exp(-0.5 * x * x) * (2.0 * math.pi) ** (-0.5)
    return x * half, half + x * density


def mean_rows(x):
    return jnp.sum(x, axis=1, keepdims=True) * (1.0 / x.shape[1])


def norm_rows(z, gain, shift):
    centre = z - mean_rows(z)
    inverse = lax.rsqrt(mean_rows(centre * centre) + epsilon)
    normed = centre * inverse
    return normed * gain + shift, normed, inverse


def norm_back(g, normed, inverse, gain):
    scaled = g * gain
    return inverse * (scaled - mean_rows(scaled) - normed * mean_rows(scaled * normed))


def dense_kernel(info_ref, bhalt_ref, *refs):
    mine, other, refs = refs[:PAIRS], refs[PAIRS : 2 * PAIRS], refs[2 * PAIRS :]
    att_refs, refs = refs[:PAIRS], refs[PAIRS:]
    emb_ref, prev_ref, gt_ref, gb_ref, scal_ref = refs[:5]
    refs = refs[5:]
    final_ref, blend_ref, rows_ref, gprev_ref, base_ref = refs[:5]
    gatt_refs = refs[5:9]
    nlow_ref, ilow_ref, gin_ref, gfeed_ref, gbranch_ref, vsum_ref, bsum_ref = refs[9:16]
    slope_ref, win_ref, wouter_ref, wout_ref, small_ref, sem = refs[16:]
    blocks, columns, width = win_ref.shape
    cut = wout_ref.shape[1] // 2
    core, zed, pair = info_ref[0], info_ref[1], info_ref[2]

    def load(firsts, seconds):
        copies = []

        def copy(source, start, size, target):
            copies.append(pltpu.make_async_copy(source.at[pl.ds(start, size)], target, sem.at[len(copies)]))

        for a in range(PAIRS):
            place = lax.rem(zed + a, PAIRS)
            order = jnp.bitwise_xor(place, pair)
            first, second = firsts[(-a) % PAIRS], seconds[a]
            copy(first, columns, cut, wout_ref.at[order, pl.ds(0, cut)])
            copy(second, width, cut, wout_ref.at[order, pl.ds(cut, cut)])
            copy(first, columns + cut, SMALL, small_ref.at[place])
            copy(first, 0, columns, win_ref.at[a])
            copy(second, 0, width, wouter_ref.at[a])
        for one in copies:
            one.start()
        for one in copies:
            one.wait()

    @pl.when((pl.program_id(0) == 0) & (core == 0))
    def _():
        load(mine, other)

    @pl.when((pl.program_id(0) == 0) & (core != 0))
    def _():
        load(other, mine)

    emb = emb_ref[0]
    att = jnp.concatenate([ref[0] for ref in att_refs], axis=1)
    w_out = wout_ref[...].reshape(emb.shape[1], emb.shape[1])
    b_outer, g1, s1, g2, s2, halt = [
        jnp.concatenate([small_ref[a, i + 1 : i + 2, :WIDE] for a in range(PAIRS)], axis=1).astype(f32)
        for i in range(6)
    ]
    cols = jnp.transpose(scal_ref[0])
    sum_col, code_col, gsum_col = cols[:, 0:1], cols[:, 1:2], cols[:, 2:3]
    z1 = emb + dot(att, w_out)
    one, n1, i1 = norm_rows(z1, g1, s1)
    nlow = one.astype(bf16)
    nlow_ref[0] = nlow
    feed = None
    for j in range(blocks):
        pre = dot(nlow, win_ref[j]) + small_ref[lax.rem(zed + j, PAIRS), 0:1, :].astype(f32)
        act, slope = gelu_parts(pre)
        act = act.astype(bf16)
        ilow_ref[0, :, j * width : (j + 1) * width] = act
        slope_ref[:, j * width : (j + 1) * width] = slope
        part = dot(act, wouter_ref[j])
        feed = part if feed is None else feed + part
    z2 = one + (feed + b_outer)
    final, n2, i2 = norm_rows(z2, g2, s2)
    halt_logit = jnp.sum(emb * halt, axis=1, keepdims=True) + bhalt_ref[0, 0]
    halt_prob = jax.nn.sigmoid(halt_logit)
    running = (code_col > 0.5).astype(f32)
    halting = (code_col > 1.5).astype(f32)
    update = running * (halting * (1.0 - sum_col) + (1.0 - halting) * halt_prob)
    prev = prev_ref[0].astype(f32)
    gb = gb_ref[0].astype(f32)
    final_ref[0] = final.astype(bf16)
    blend_ref[0] = (prev * (1.0 - update) + final * update).astype(bf16)
    gprev_ref[0] = gb * (1.0 - update)
    g_update = jnp.sum(gb * (final - prev), axis=1, keepdims=True) + gsum_col
    g_halt_sum = gsum_col - running * halting * g_update
    g_logit = g_update * running * (1.0 - halting) * halt_prob * (1.0 - halt_prob)
    lane = lax.broadcasted_iota(jnp.int32, (emb.shape[0], WIDE), 1)
    packed = jnp.where(lane == 0, sum_col + update, jnp.where(lane == 1, g_halt_sum, 0.0))
    rows_ref[0] = jnp.transpose(packed)[0:8]
    gf = gt_ref[0].astype(f32) + update * gb
    g_two = norm_back(gf, n2, i2, g2)
    gfeed = g_two.astype(bf16)
    gfeed_ref[0] = gfeed
    g_one = g_two
    for j in range(blocks):
        at = slice(j * width, (j + 1) * width)
        back = dot(gfeed, wouter_ref[j], NT)
        gin_f = back * slope_ref[:, at]
        gin = gin_f.astype(bf16)
        gin_ref[0, :, at] = gin
        bsum_ref[0, :, at] = jnp.sum(gin.astype(f32), axis=0, keepdims=True)
        g_one = g_one + dot(gin, win_ref[j], NT)
    g_emb = norm_back(g_one, n1, i1, g1)
    gbranch = g_emb.astype(bf16)
    gbranch_ref[0] = gbranch
    gatt = dot(gbranch, w_out, NT).astype(bf16)
    for d, ref in enumerate(gatt_refs):
        ref[0] = gatt[:, d * WIDE : (d + 1) * WIDE]
    base_ref[0] = g_emb + g_logit * halt
    total = lambda x: jnp.sum(x, axis=0, keepdims=True)
    logit_sum = jnp.broadcast_to(total(g_logit), (1, emb.shape[1]))
    vsum_ref[0] = jnp.concatenate(
        [
            total(gfeed.astype(f32)),
            total(g_one * n1),
            total(g_one),
            total(gf * n2),
            total(gf),
            total(g_logit * emb),
            logit_sum,
            jnp.zeros((1, emb.shape[1]), f32),
        ],
        axis=0,
    )


def dense(info, b_halt, mine, other, emb, att, prev, gt, gb, scal, part, out_rows):
    seqs, rows, width = emb.shape
    hidden = PAIRS * part
    anywhere = pl.BlockSpec(memory_space=pl.ANY)
    scalars = pl.BlockSpec(memory_space=pltpu.SMEM)
    rowspec = lambda w: pl.BlockSpec((1, rows, w), lambda s: (s, 0, 0))
    shape = lambda w, kind: jax.ShapeDtypeStruct((seqs, rows, w), kind)
    return pl.pallas_call(
        dense_kernel,
        grid=(seqs,),
        in_specs=[scalars, scalars]
        + [anywhere] * (2 * PAIRS)
        + [rowspec(WIDE)] * PAIRS
        + [
            rowspec(width),
            rowspec(width),
            rowspec(width),
            rowspec(width),
            pl.BlockSpec((1, 8, rows), lambda s: (s, 0, 0)),
        ],
        out_specs=[
            rowspec(width),
            rowspec(width),
            pl.BlockSpec((1, 8, rows), lambda s: (s, 0, 0)),
            rowspec(width),
            rowspec(width),
            rowspec(WIDE),
            rowspec(WIDE),
            rowspec(WIDE),
            rowspec(WIDE),
            rowspec(width),
            rowspec(hidden),
            rowspec(hidden),
            rowspec(width),
            rowspec(width),
            pl.BlockSpec((1, 8, width), lambda s: (s, 0, 0)),
            pl.BlockSpec((1, 1, hidden), lambda s: (s, 0, 0)),
        ],
        out_shape=[
            shape(width, bf16),
            shape(width, bf16),
            jax.ShapeDtypeStruct((seqs, 8, rows), f32),
            shape(width, f32),
            shape(width, f32),
            shape(WIDE, bf16),
            shape(WIDE, bf16),
            shape(WIDE, bf16),
            shape(WIDE, bf16),
            shape(width, bf16),
            shape(hidden, bf16),
            shape(hidden, bf16),
            shape(width, bf16),
            shape(width, bf16),
            jax.ShapeDtypeStruct((seqs, 8, width), f32),
            jax.ShapeDtypeStruct((seqs, 1, hidden), f32),
        ],
        scratch_shapes=[
            pltpu.VMEM((rows, hidden), f32),
            pltpu.VMEM((PAIRS, width, part), bf16),
            pltpu.VMEM((PAIRS, part, width), bf16),
            pltpu.VMEM((PAIRS, out_rows, width), bf16),
            pltpu.VMEM((PAIRS, SMALL, width), bf16),
            pltpu.SemaphoreType.DMA((5 * PAIRS,)),
        ],
        compiler_params=room(56),
        cost_estimate=cost(20),
        name="dense",
    )(info, b_halt, *mine, *other, *att, emb, prev, gt, gb, scal)


def frequencies(half):
    return jnp.exp(-math.log(10000.0) * jnp.arange(half, dtype=f32) / (half - 1))


def position_rows(first, rows, columns):
    half = columns // 2
    freq = frequencies(half)[None, :]
    coarse = (first + 16 * jnp.arange(rows // 16, dtype=jnp.int32)).astype(f32)[:, None] * freq
    fine = jnp.arange(16, dtype=f32)[:, None] * freq
    sa, ca = jnp.sin(coarse)[:, None], jnp.cos(coarse)[:, None]
    sb, cb = jnp.sin(fine)[None], jnp.cos(fine)[None]
    both = jnp.concatenate([sa * cb + ca * sb, ca * cb - sa * sb], axis=2)
    return both.reshape(rows, columns)


def step_rows(columns):
    half = columns // 2
    angles = jnp.arange(4, dtype=f32)[:, None] * frequencies(half)[None, :]
    return jnp.concatenate([jnp.sin(angles), jnp.cos(angles)], axis=1)


def body(
    hidden_state,
    prev_state,
    halt_sum,
    halt_code,
    step_count,
    w_query,
    w_key,
    w_value,
    w_out,
    w_inner,
    b_inner,
    w_outer,
    b_outer,
    gain_attention,
    shift_attention,
    gain_feedforward,
    shift_feedforward,
    w_halt,
    b_halt,
    grad_transformed,
    grad_blended,
    grad_sum,
):
    seqs, rows, width = hidden_state.shape
    ctx = lax.axis_size("ctx")
    wsh = lax.axis_size("wsh")
    repeats = ctx // (2 * PAIRS)
    me = lax.axis_index("ctx")
    zed = lax.axis_index("wsh")
    core = me % 2
    pair = (me // 2) % PAIRS

    def swap(x, distance):
        return lax.ppermute(x, "ctx", [(i, i ^ distance) for i in range(ctx)])

    def sibling(x):
        return swap(x, 1)

    def partners(x, distance):
        return swap(x, 2 * distance)

    freq_rows = position_rows(me * rows, rows, width)
    table = step_rows(width)
    steps = step_count[:, :, None]
    step_signal = jnp.where(
        steps == 0, table[0], jnp.where(steps == 1, table[1], jnp.where(steps == 2, table[2], table[3]))
    )
    emb = hidden_state.astype(f32) + freq_rows[None] + step_signal
    emb_low = emb.astype(bf16)

    after = lambda x, *others: lax.optimization_barrier((x,) + others)[0]

    info = jnp.stack([core, zed, pair]).astype(jnp.int32)
    ring = [
        (c * wsh + z, c * wsh + (z + (1 if c % 2 == 0 else -1)) % wsh) for c in range(ctx) for z in range(wsh)
    ]
    turn = lambda x: lax.ppermute(x, ("ctx", "wsh"), ring)
    out_rows = w_out.shape[0]
    part = w_inner.shape[1]
    half = rows // 2

    mine = [pack(info, [w_query, w_key, w_value])]
    mine.append(turn(mine[0]))
    mine.append(turn(after(mine[1], emb_low)))
    tokens = [emb_low] + [partners(emb_low, d) for d in (1, 2)]
    mine.append(turn(after(mine[2], *tokens[1:])))
    tokens.append(partners(tokens[2][:, :half], 1))
    tokens.append(partners(tokens[1][:, half:], 2))
    other = [sibling(x) for x in mine]
    vectors = [b_outer, gain_attention, shift_attention, gain_feedforward, shift_feedforward, w_halt]
    feed = pack_feed(after(info, mine[0]), w_inner, w_outer, w_out, b_inner, vectors)
    feed_mine = [feed, turn(after(feed, mine[1]))]
    w_order = assemble(after(info, feed_mine[1]), mine, other)

    groups = [[r * 2 * PAIRS + i for r in range(repeats)] for i in range(2 * PAIRS)]
    q_list, kvs_list, fold = [], [], None
    w_now = w_order
    for s in range(seqs):
        q, own = project(s, tokens, w_now)
        w_now = after(w_order, q)
        other = sibling(own)
        if repeats == 1:
            kvs = [own, other]
        else:
            both = jnp.concatenate([own, other], axis=1)
            kvs = [lax.all_gather(both, "ctx", axis=1, tiled=True, axis_index_groups=groups)]
        q_list.append(q)
        kvs_list.append(kvs)
    feed_mine.append(turn(after(feed_mine[1], q_list[0])))
    feed_other = [sibling(after(x, q_list[0])) for x in feed_mine[:2]]
    fold = attend(0, seqs, q_list[0], kvs_list[0], None)
    fold = attend(1, seqs, after(q_list[1], *feed_other, fold[1]), kvs_list[1], fold)
    feed_mine.append(turn(after(feed_mine[2], fold[1])))
    fold = attend(2, seqs, after(q_list[2], feed_mine[2]), kvs_list[2], fold)
    feed_other += [sibling(after(x, fold[1])) for x in feed_mine[2:]]
    o32, mass, *low = fold
    att = [low[0]] + [partners(low[d], d) for d in range(1, PAIRS)]

    zero_row = jnp.zeros_like(halt_sum)
    scal = jnp.stack([halt_sum, halt_code.astype(f32), grad_sum] + [zero_row] * 5, axis=1)
    (
        final,
        blended,
        row_out,
        grad_prev,
        base,
        gatt0,
        gatt1,
        gatt2,
        gatt3,
        nlow,
        ilow,
        gin,
        gfeed,
        gbranch,
        vsum,
        bsum,
    ) = dense(
        info, b_halt.reshape(1, 1), feed_mine, feed_other, emb, att, prev_state, grad_transformed, grad_blended,
        scal, part, out_rows,
    )
    new_sum = row_out[:, 0]
    grad_halt_sum = row_out[:, 1]
    gs = [gatt0] + [partners(x, d + 1) for d, x in enumerate((gatt1, gatt2, gatt3))]

    keep_a, give_a = outer_grads(info, att, ilow, gfeed, gbranch, ctx)
    keep_b, give_b = inner_grads(after(info, keep_a), nlow, gin, vsum, bsum, ctx)
    joined_a = join(after(keep_a, keep_b), sibling(give_a), False)

    def spread_pieces(pieces):
        return [pieces[0]] + [partners(pieces[d], d) for d in range(1, PAIRS)]

    shared_a = spread_pieces(joined_a)

    kinds = [f32, bf16] if repeats == 1 else [bf16]

    def split_back(s, token):
        dq, *dkv = attend_back(s, q_list[s], gs, o32, token, kvs_list[s], kinds)
        if repeats == 1:
            kept, sent = dkv
        else:
            summed = lax.psum_scatter(
                dkv[0], "ctx", scatter_dimension=1, tiled=True, axis_index_groups=groups
            )
            kept, sent = summed[:, : PAIRS * rows].astype(f32), summed[:, PAIRS * rows :]
        return dq, kept, sibling(sent)

    backs = [split_back(0, after(mass, *joined_a))]
    joined_b = join(after(keep_b, backs[0][0], *shared_a), sibling(give_b), True)
    shared_b = spread_pieces(joined_b)
    backs.append(split_back(1, after(mass, *joined_b)))
    *pieces, gq = combine(after(info, backs[1][0], *shared_b), (0,), tokens, backs[:1], None, False)
    blocks = [spread_pieces(pieces)]
    share_keep, share_send = share_parts(after(info, gq), shared_a, shared_b)
    if repeats > 1:
        share_keep, share_send = (
            lax.psum_scatter(x, "ctx", scatter_dimension=0, tiled=True, axis_index_groups=groups)
            for x in (share_keep, share_send)
        )
    cross = lambda x, step: lax.ppermute(x, "wsh", [(z, z ^ step) for z in range(wsh)])
    moved = cross(share_send[0], 1)
    backs.append(split_back(2, after(mass, share_keep)))
    own, sent = halve(after(share_keep[0], backs[2][0], *blocks[0]), moved)
    moved = cross(sent, 2)
    made = combine(after(info, own), (1, 2), tokens, backs[1:], gq, repeats == 1)
    pieces, keep, give = made[:PAIRS], made[PAIRS], made[-1]
    block = [pieces[0]] + [partners(pieces[d], d) for d in (1, 2)]
    if repeats == 1:
        heads = share_small(after(info, moved, *block), spread_pieces(join_small(keep, sibling(give))))
        block.append(partners(after(pieces[3], heads[0]), 3))
        heads = [heads[0]] + [cross(heads[step], step) for step in range(1, wsh)]
        share = total_parts([own, moved], heads)
        mine = spread_pieces([share] * PAIRS)
        (grad_w_outer, grad_w_out, grad_w_inner, tail, grad_w_query, grad_w_key, grad_w_value) = unpack(
            info, mine, [sibling(x) for x in mine], part, out_rows
        )
    else:
        block.append(partners(pieces[3], 3))
        share = total_parts([own, moved], [])
        whole = lax.all_gather(share, "ctx", axis=0).astype(f32)
        a, b, c = part // ctx, out_rows // ctx, width // ctx
        grad_w_outer = whole[:, :a].reshape(part, width)
        grad_w_out = whole[:, a : a + b].reshape(out_rows, width)
        grad_w_inner = whole[:, a + b : a + b + c].reshape(width, part)
        tail = whole[0, a + b + c :]
        own = lax.dynamic_update_index_in_dim(jnp.zeros((wsh,) + keep.shape, f32), keep, pair, 0)
        own = lax.psum(lax.psum_scatter(own.astype(bf16), "wsh", scatter_dimension=0).astype(f32), "ctx")
        grad_w_query, grad_w_key, grad_w_value = (own[:, i * WIDE : (i + 1) * WIDE] for i in range(3))
    blocks.append(block)
    grad_state = base
    for s in range(seqs):
        block, place = (blocks[0], 0) if s == 0 else (blocks[1], s - 1)
        grad_state = add_state(s, place, grad_state, block, w_order)

    grad_b_inner = tail[7]
    vec_grads = [tail[i, :out_rows] for i in range(6)]
    grad_b_halt = tail[6, :1] + tail[6, WIDE : WIDE + 1]

    return (
        final,
        blended,
        new_sum,
        grad_state,
        grad_prev,
        grad_halt_sum,
        grad_w_query,
        grad_w_key,
        grad_w_value,
        grad_w_out,
        grad_w_inner,
        grad_b_inner,
        grad_w_outer,
        vec_grads[0],
        vec_grads[1],
        vec_grads[2],
        vec_grads[3],
        vec_grads[4],
        vec_grads[5],
        grad_b_halt,
    )


def solution(mesh):
    rows = P("wsh", "ctx", None)
    marks = P("wsh", "ctx")
    column, row, vector = P(None, "wsh"), P("wsh", None), P("wsh")
    in_specs = (
        (rows, rows, marks, marks, marks, column, column, column, row, column, vector, row)
        + (vector,) * 6
        + (P(), rows, rows, marks)
    )
    out_specs = (
        (rows, rows, marks, rows, rows, marks, column, column, column, row, column, vector, row)
        + (vector,) * 6
        + (P(),)
    )
    return jax.shard_map(body, mesh=mesh, in_specs=in_specs, out_specs=out_specs, check_vma=False)
```

time: 979 us -> 272 us (0.28)
  waiting for transfers between devices: 360 us -> 82.3 us
  matrix products: 175 us -> 0 us
  blocking collectives: 156 us -> 0 us
  other arithmetic: 142 us -> 2.68 us
  Pallas kernels: 0 us -> 116 us
  local copies, waits for them, and re-layouts: 110 us -> 13.5 us
  starting transfers between devices: 1.33 us -> 52.1 us
  between operations: 22.8 us -> 4.83 us
    reduce_scatter x9 -> x0, waiting for transfers between devices: 253 us -> none  [the longest x3 129 us: run_batch(): lax.psum_scatter(grad_keys.astype(jnp.bfloat16), 'ctx', scatter_dimension...]
    dot_general x144 -> x0, matrix products: 175 us -> none  [the longest x12 33 us: attend_sweep(): jnp.einsum('qhd,khd->hqk', query_heads, key_part, preferred_element_type=...]
    all_gather x11 -> x0, blocking collectives: 124 us -> none  [the longest x1 16.9 us: body(): lax.all_gather(w_key, 'wsh', axis=1, tiled=True)]
    pallas_call x0 -> x28, Pallas kernels: none -> 116 us  [the longest x3 39.4 us: attend_back(): pl.pallas_call(functools.partial(attend_back_kernel, len(kvs)), grid=(1,)...]
    ppermute x0 -> x60, waiting for transfers between devices: none -> 82.3 us  [the longest x49 39.6 us: swap(): return lax.ppermute(x, 'ctx', [(i, i ^ distance) for i in range(ctx)])]
    psum x1 -> x0, waiting for transfers between devices: 62 us -> none  [body(): lax.psum(shares[0].astype(jnp.bfloat16), 'ctx').astype(jnp.float32)]
    ppermute x0 -> x60, starting transfers between devices: none -> 52.1 us  [the longest x49 41.7 us: swap(): return lax.ppermute(x, 'ctx', [(i, i ^ distance) for i in range(ctx)])]
    reduce_sum x27 -> x0, other arithmetic: 45.8 us -> none  [the longest x12 36.5 us: attend_sweep(): row_mass = row_mass * factor + jnp.sum(exponent, axis=2)]
  transfers between devices with their start and end apart: 21 -> 60, of which waited for: 10 -> 18; matrix products, arithmetic and copies ran while one was open for 29% -> 2% of each run, Pallas kernels for 0% -> 31%
where the time goes in v1:
time: 272 us; the launch traced here: 271 us
  Pallas kernels  116 us (43%)
  waiting for transfers between devices  82.3 us (30%)
  starting transfers between devices  52.1 us (19%)
  local copies, waits for them, and re-layouts  13.5 us (5%)
  between operations  4.83 us (2%)
    ppermute x49, starting transfers between devices, swap(): return lax.ppermute(x, 'ctx', [(i, i ^ distance) for i in range(ctx)])  41.7 us
    ppermute x49, waiting for transfers between devices, swap(): return lax.ppermute(x, 'ctx', [(i, i ^ distance) for i in range(ctx)])  39.6 us
    pallas_call x3, Pallas kernels, attend_back(): pl.pallas_call(functools.partial(attend_back_kernel, len(kvs)), grid=(1,)...  39.4 us
    ppermute x6, waiting for transfers between devices, body(): turn = lambda x: lax.ppermute(x, ('ctx', 'wsh'), ring)  33.2 us
    pallas_call x3, Pallas kernels, attend(): pl.pallas_call(functools.partial(attend_kernel, len(kvs), carried), grid=...  26.5 us
    pallas_call x1, Pallas kernels, dense(): pl.pallas_call(dense_kernel, grid=(seqs,), in_specs=[scalars, scalars] +...  19.8 us
    ppermute x5, waiting for transfers between devices, body(): lax.ppermute(x, 'wsh', [(z, z ^ step) for z in range(wsh)])  9.58 us
    pallas_call x2, Pallas kernels, split_grads(): pl.pallas_call(kernel, grid_spec=pltpu.PrefetchScalarGridSpec(num_scalar_...  9.52 us
  transfers between devices with their start and end apart: 60, of which 18 were waited for; matrix products, arithmetic and copies ran while one was open for 2% of the time, Pallas kernels for 31%

profile of v1, /device:TPU:0, one launch (start us, length us, event | category | flops | bytes accessed | tf_op | source)
XLA Modules:
  0.0 271.2 jit_solution(11328452384672162503)
XLA Ops:
  1.9 1.5 select_add_fusion
  3.4 3.0 %collective-permute-start.3 = (bf16[3,256,512]{2,1,0:T(8,128)(2,1)S(1)}, bf16[3,256,512]{2,1,0:T(8,128)(2,1)S(1)}, u32[]{:S(2)}, u32[]{:S(2)}) collective-permute-start(bf16[3,256,512]{2,1,0:T(8,128)(2,1)S(1)} %get-tuple-element.255.refs_0_), channel_id=1, source_target_pairs={{0,16},{4,20},{8,24},{12,28},{16,0},{20,4},{24,8},{28,12},{1,17},{... | collective-permute-start | bytes 2359304 | tf_op jit(solution)/shard_map/ppermute | solution.py:980
  6.3 1.5 collective-permute-start.2
  8.6 1.6 collective-permute-start
  11.0 5.8 %collective-permute-done.refs_1_ = bf16[256,384]{1,0:T(8,128)(2,1)S(1)} collective-permute-done((bf16[256,384]{1,0:T(8,128)(2,1)S(1)}, bf16[256,384]{1,0:T(8,128)(2,1)S(1)}, u32[]{:S(2)}, u32[]{:S(2)}) %collective-permute-start) | collective-permute-done | bytes 196640 | tf_op jit(solution)/shard_map/ppermute | solution.py:1003
  17.7 1.9 collective-permute-start.6
  19.6 18.2 %collective-permute-done.6.refs_2_ = bf16[256,384]{1,0:T(8,128)(2,1)S(1)} collective-permute-done((bf16[256,384]{1,0:T(8,128)(2,1)S(1)}, bf16[256,384]{1,0:T(8,128)(2,1)S(1)}, u32[]{:S(2)}, u32[]{:S(2)}) %collective-permute-start.6) | collective-permute-done | bytes 196640 | tf_op jit(solution)/shard_map/ppermute | solution.py:1003
  38.0 2.0 collective-permute-start.8
  40.5 4.8 %collective-permute-done.7.refs_3_ = bf16[256,384]{1,0:T(8,128)(2,1)S(1)} collective-permute-done((bf16[256,384]{1,0:T(8,128)(2,1)S(1)}, bf16[256,384]{1,0:T(8,128)(2,1)S(1)}, u32[]{:S(2)}, u32[]{:S(2)}) %collective-permute-start.7) | collective-permute-done | bytes 196640 | tf_op jit(solution)/shard_map/ppermute | solution.py:1003
  47.6 9.5 %collective-permute-done.4.refs_3_ = bf16[3,128,512]{2,1,0:T(8,128)(2,1)S(1)} collective-permute-done((bf16[3,128,512]{2,1,0:T(8,128)(2,1)S(1)}, bf16[3,128,512]{2,1,0:T(8,128)(2,1)S(1)}, u32[]{:S(2)}, u32[]{:S(2)}) %collective-permute-start.4) | collective-permute-done | bytes 393248 | tf_op jit(solution)/shard_map/ppermute | solution.py:980
  61.0 2.8 %collective-permute-start.18 = (bf16[1,1024,256]{2,1,0:T(8,128)(2,1)S(1)}, bf16[1,1024,256]{2,1,0:T(8,128)(2,1)S(1)}, u32[]{:S(2)}, u32[]{:S(2)}) collective-permute-start(bf16[1,1024,256]{2,1,0:T(8,128)(2,1)S(1)} %get-tuple-element.161.refs_0_.refs_6_), channel_id=1, source_target_pairs={{0,4},{4,0},{8,12},{12,8},{16,20},{20,16},{24,28},{28,24},{1,5},{5... | collective-permute-start | bytes 1572872 | tf_op jit(solution)/shard_map/ppermute | solution.py:980
  63.8 8.8 %attend.3 = (f32[3,1024,128]{2,1,0:T(8,128)S(1)}, f32[3,8,1024]{2,1,0:T(8,128)S(1)}, bf16[3,256,128]{2,1,0:T(8,128)(2,1)S(1)}, bf16[3,256,128]{2,1,0:T(8,128)(2,...) custom-call(bf16[1,1024,128]{2,1,0:T(8,128)(2,1)S(1)} %get-tuple-element.142.q_ref, ...), custom_call_target="tpu_custom_call" | custom-call | flops 4400000000 | bytes 1024 | tf_op jit(solution)/shard_map/attend/pallas_call | solution.py:95
  72.7 8.8 %attend.4 = (f32[3,1024,128]{2,1,0:T(8,128)S(1)}, f32[3,8,1024]{2,1,0:T(8,128)S(1)}, bf16[3,256,128]{2,1,0:T(8,128)(2,1)S(1)}, bf16[3,256,128]{2,1,0:T(8,128)(2,...) custom-call(bf16[1,1024,128]{2,1,0:T(8,128)(2,1)S(1)} %get-tuple-ele, ...), custom_call_target="tpu_custom_call", output_to_operand_aliasing={{0}: (3, {}), {1}: (4, {}), {2}: (5, {}), {3}: (6, {}), {4}... | custom-call | flops 4400000000 | bytes 1024 | tf_op jit(solution)/shard_map/attend/pallas_call | solution.py:95
  81.9 8.8 %attend.5 = (f32[3,1024,128]{2,1,0:T(8,128)S(1)}, f32[3,8,1024]{2,1,0:T(8,128)S(1)}, bf16[3,256,128]{2,1,0:T(8,128)(2,1)S(1)}, bf16[3,256,128]{2,1,0:T(8,128)(2,...) custom-call(bf16[1,1024,128]{2,1,0:T(8,128)(2,1)S(1)} %get-tuple-ele, ...), custom_call_target="tpu_custom_call", output_to_operand_aliasing={{0}: (3, {}), {1}: (4, {}), {2}: (5, {}), {3}: (6, {}), {4}... | custom-call | flops 4400000000 | bytes 1024 | tf_op jit(solution)/shard_map/attend/pallas_call | solution.py:95
  94.2 4.3 %collective-permute-done.17.refs_3_ = bf16[592,512]{1,0:T(8,128)(2,1)} collective-permute-done((bf16[592,512]{1,0:T(8,128)(2,1)}, bf16[592,512]{1,0:T(8,128)(2,1)}, u32[]{:S(2)}, u32[]{:S(2)}) %collective-permute-start.17) | collective-permute-done | bytes 606240 | tf_op jit(solution)/shard_map/ppermute | solution.py:1003
  98.4 1.5 collective-permute-start.21
  100.4 1.5 collective-permute-start.23
  106.4 5.0 %collective-permute-done.22.refs_10_.a2_ref = bf16[3,256,128]{2,1,0:T(8,128)(2,1)} collective-permute-done((bf16[3,256,128]{2,1,0:T(8,128)(2,1)}, bf16[3,256,128]{2,1,0:T(8,128)(2,1)}, u32[]{:S(2)}, u32[]{:S(2)}) %collective-permute-start.22) | collective-permute-done | bytes 196640 | tf_op jit(solution)/shard_map/ppermute | solution.py:980
  111.5 19.8 %dense.1 = (bf16[3,256,512]{2,1,0:T(8,128)(2,1)}, bf16[3,256,512]{2,1,0:T(8,128)(2,1)}, f32[3,8,256]{2,1,0:T(8,128)}, f32[3,256,512]{2,1,0:T(8,128)}, f32[3,256,...) custom-call(s32[3]{0:T(128)} %copy-done.5, ...), custom_call_target="tpu_custom_call" | custom-call | flops 22000001024 | bytes 1024 | tf_op jit(solution)/shard_map/dense/pallas_call | solution.py:862
  131.3 1.9 copy-done.38
  135.5 5.7 %outer_grads.1 = (bf16[4,1,4,80,512]{4,3,2,1,0:T(8,128)(2,1)S(1)}, bf16[4,1,4,80,512]{4,3,2,1,0:T(8,128)(2,1)S(1)}) custom-call(s32[3]{0:T(128)S(1)} %copy-done.6, bf16[3,256,128]{2,1,0:T(8,128)(2,1)S(1)} %copy-done.46, bf16[3,256,128]{2,1,0:T(8,128)(2,1)} %collective-permute-done.21.refs_9_.a1_ref, ...), custom_call_target="tpu_custom_call" | custom-call | flops 4950000128 | bytes 1024 | tf_op jit(solution)/shard_map/outer_grads/pallas_call | solution.py:522
  143.1 1.8 collective-permute-start.26
  144.9 3.8 %inner_grads.1 = (bf16[4,1,4,72,512]{4,3,2,1,0:T(8,128)(2,1)S(1)}, bf16[4,1,4,72,512]{4,3,2,1,0:T(8,128)(2,1)S(1)}) custom-call(s32[3]{0:T(128)S(1)} %copy-done.6, bf16[3,256,512]{2,1,0:T(8,128)(2,1)S(1)} %copy-done.44, bf16[3,256,2048]{2,1,0:T(8,128)(2,1)S(1)} %copy-done.39, f32[3,8,512]{2,1,0:T(8,128)S(1)} %copy-done.49, f32[3,1,2048]{2,1,0:T(1,128)S(1)} %copy-done.50), custom_call_target="tpu_custom_call" | custom-call | flops 4950000128 | bytes 1024 | tf_op jit(solution)/shard_map/inner_grads/pallas_call | solution.py:522
  151.2 1.9 collective-permute-done.25.refs_2_
  153.2 1.4 collective-permute-start.30
  154.6 13.3 %attend_back.3 = (bf16[1,1024,128]{2,1,0:T(8,128)(2,1)S(1)}, f32[1,1024,256]{2,1,0:T(8,128)S(1)}, bf16[1,1024,256]{2,1,0:T(8,128)(2,1)S(1)}) custom-call(bf16[1,1024,128]{2,1,0:T(8,128)(2,1)S(1)} %copy-done.27, bf16[3,256,128]{2,1,0:T(8,128)(2,1)S(1)} %copy-done.51, bf16[3,256,128]{2,1,0:T(8,128)(2,1)S(1)} %collective-permute-done.24.refs_1_, ...), custom_call_target="tpu_custom_call" | custom-call | flops 15399999488 | bytes 1024 | tf_op jit(solution)/shard_map/attend_back/pallas_call | solution.py:176
  169.3 1.5 collective-permute-start.33
  170.8 1.4 collective-permute-start.34
  172.2 13.1 %attend_back.4 = (bf16[1,1024,128]{2,1,0:T(8,128)(2,1)S(1)}, f32[1,1024,256]{2,1,0:T(8,128)S(1)}, bf16[1,1024,256]{2,1,0:T(8,128)(2,1)S(1)}) custom-call(bf16[1,1024,128]{2,1,0:T(8,128)(2,1)S(1)} %copy-done.25, bf16[3,256,128]{2,1,0:T(8,128)(2,1)S(1)} %copy-done.51, bf16[3,256,128]{2,1,0:T(8,128)(2,1)S(1)} %collective-permute-done.24.refs_1_, ...), custom_call_target="tpu_custom_call" | custom-call | flops 15399999488 | bytes 1024 | tf_op jit(solution)/shard_map/attend_back/pallas_call | solution.py:176
  188.2 13.1 %attend_back.5 = (bf16[1,1024,128]{2,1,0:T(8,128)(2,1)S(1)}, f32[1,1024,256]{2,1,0:T(8,128)S(1)}, bf16[1,1024,256]{2,1,0:T(8,128)(2,1)S(1)}) custom-call(bf16[1,1024,128]{2,1,0:T(8,128)(2,1)S(1)} %copy-done.23, bf16[3,256,128]{2,1,0:T(8,128)(2,1)S(1)} %copy-done.51, bf16[3,256,128]{2,1,0:T(8,128)(2,1)S(1)} %collective-permute-done.24.refs_1_, ...), custom_call_target="tpu_custom_call" | custom-call | flops 15399999488 | bytes 1024 | tf_op jit(solution)/shard_map/attend_back/pallas_call | solution.py:176
  202.3 1.5 collective-permute-start.37
  203.8 4.8 %collective-permute-done.36.refs_1_ = bf16[1,256,384]{2,1,0:T(8,128)(2,1)S(1)} collective-permute-done((bf16[1,256,384]{2,1,0:T(8,128)(2,1)S(1)}, bf16[1,256,384]{2,1,0:T(8,128)(2,1)S(1)}, u32[]{:S(2)}, u32[]{:S(2)}) %collective-permute-start.36) | collective-permute-done | bytes 196640 | tf_op jit(solution)/shard_map/ppermute | solution.py:980
  208.6 1.8 collective-permute-start.38
  210.4 5.2 %collective-permute-done.38.refs_3_ = bf16[1,256,384]{2,1,0:T(8,128)(2,1)S(1)} collective-permute-done((bf16[1,256,384]{2,1,0:T(8,128)(2,1)S(1)}, bf16[1,256,384]{2,1,0:T(8,128)(2,1)S(1)}, u32[]{:S(2)}, u32[]{:S(2)}) %collective-permute-start.38) | collective-permute-done | bytes 196640 | tf_op jit(solution)/shard_map/ppermute | solution.py:980
  215.8 2.3 combine.3
  219.0 1.8 collective-permute-start.43
  223.1 7.2 %collective-permute-done.44.refs_1_ = bf16[152,512]{1,0:T(8,128)(2,1)S(1)} collective-permute-done((bf16[152,512]{1,0:T(8,128)(2,1)S(1)}, bf16[152,512]{1,0:T(8,128)(2,1)S(1)}, u32[]{:S(2)}, u32[]{:S(2)}) %collective-permute-start.44) | collective-permute-done | bytes 155680 | tf_op jit(solution)/shard_map/ppermute | solution.py:1106
  232.2 3.1 %collective-permute-done.48.refs_3_ = bf16[64,384]{1,0:T(8,128)(2,1)S(1)} collective-permute-done((bf16[64,384]{1,0:T(8,128)(2,1)S(1)}, bf16[64,384]{1,0:T(8,128)(2,1)S(1)}, u32[]{:S(2)}, u32[]{:S(2)}) %collective-permute-start.48) | collective-permute-done | bytes 49184 | tf_op jit(solution)/shard_map/ppermute | solution.py:980
  236.0 2.5 collective-permute-start.51
  238.5 1.9 collective-permute-start.52
  242.0 2.4 collective-permute-done.52.refs_5_
  245.4 1.6 collective-permute-start.54
  248.0 2.6 add_state.3.base_ref
  250.6 6.4 %collective-permute-done.55.refs_3_ = bf16[200,512]{1,0:T(8,128)(2,1)S(1)} collective-permute-done((bf16[200,512]{1,0:T(8,128)(2,1)S(1)}, bf16[200,512]{1,0:T(8,128)(2,1)S(1)}, u32[]{:S(2)}, u32[]{:S(2)}) %collective-permute-start.55) | collective-permute-done | bytes 204832 | tf_op jit(solution)/shard_map/ppermute | solution.py:980
  257.0 2.1 collective-permute-done.54.refs_2_
  259.6 2.6 add_state.4.base_ref
  262.2 2.6 add_state.5
  264.8 2.4 unpack.1
  (251 shorter events, 41.6 us)
Async XLA Ops:
  3.4 34.5 %collective-permute-start.3 = (bf16[3,256,512]{2,1,0:T(8,128)(2,1)S(1)}, bf16[3,256,512]{2,1,0:T(8,128)(2,1)S(1)}, u32[]{:S(2)}, u32[]{:S(2)}) collective-permute-start(bf16[3,256,512]{2,1,0:T(8,128)(2,1)S(1)} %get-tuple-element.255.refs_0_), channel_id=1, source_target_pairs={{0,16},{4,20},{8,24},{12,28},{16,0},{20,4},{24,8},{28,12},{1,17},{... | collective-permute-start | bytes 2359304 | tf_op jit(solution)/shard_map/ppermute | solution.py:980
  6.3 31.5 %collective-permute-start.2 = (bf16[3,256,512]{2,1,0:T(8,128)(2,1)S(1)}, bf16[3,256,512]{2,1,0:T(8,128)(2,1)S(1)}, u32[]{:S(2)}, u32[]{:S(2)}) collective-permute-start(bf16[3,256,512]{2,1,0:T(8,128)(2,1)S(1)} %get-tuple-element.255.refs_0_), channel_id=1, source_target_pairs={{0,8},{4,12},{8,0},{12,4},{16,24},{20,28},{24,16},{28,20},{1,9},{5... | collective-permute-start | bytes 2359304 | tf_op jit(solution)/shard_map/ppermute | solution.py:980
  8.6 8.2 %collective-permute-start = (bf16[256,384]{1,0:T(8,128)(2,1)S(1)}, bf16[256,384]{1,0:T(8,128)(2,1)S(1)}, u32[]{:S(2)}, u32[]{:S(2)}) collective-permute-start(bf16[256,384]{1,0:T(8,128)(2,1)S(1)} %pack.1.refs_0_), channel_id=1, source_target_pairs={{0,1},{1,2},{2,3},{3,0},{4,7},{5,4},{6,5},{7,6},{8,9},{9,10},{10,1... | collective-permute-start | bytes 589832 | tf_op jit(solution)/shard_map/ppermute | solution.py:1003
  16.8 29.3 %collective-permute-start.1 = (bf16[592,512]{1,0:T(8,128)(2,1)S(1)}, bf16[592,512]{1,0:T(8,128)(2,1)S(1)}, u32[]{:S(2)}, u32[]{:S(2)}) collective-permute-start(bf16[592,512]{1,0:T(8,128)(2,1)S(1)} %pack_feed.1.refs_0_), channel_id=1, source_target_pairs={{0,1},{1,2},{2,3},{3,0},{4,7},{5,4},{6,5},{7,6},{8,9},{9,10},{10,1... | collective-permute-start | bytes 1818632 | tf_op jit(solution)/shard_map/ppermute | solution.py:1003
  17.7 20.1 %collective-permute-start.6 = (bf16[256,384]{1,0:T(8,128)(2,1)S(1)}, bf16[256,384]{1,0:T(8,128)(2,1)S(1)}, u32[]{:S(2)}, u32[]{:S(2)}) collective-permute-start(bf16[256,384]{1,0:T(8,128)(2,1)S(1)} %collective-permute-done.refs_1_), channel_id=1, source_target_pairs={{0,1},{1,2},{2,3},{3,0},{4,7},{5,4},{6,5},{7,6},{8,9},{9,10},{10,1... | collective-permute-start | bytes 589832 | tf_op jit(solution)/shard_map/ppermute | solution.py:1003
  37.9 7.5 %collective-permute-start.7 = (bf16[256,384]{1,0:T(8,128)(2,1)S(1)}, bf16[256,384]{1,0:T(8,128)(2,1)S(1)}, u32[]{:S(2)}, u32[]{:S(2)}) collective-permute-start(bf16[256,384]{1,0:T(8,128)(2,1)S(1)} %collective-permute-done.6.refs_2_), channel_id=1, source_target_pairs={{0,1},{1,2},{2,3},{3,0},{4,7},{5,4},{6,5},{7,6},{8,9},{9,10},{10,1... | collective-permute-start | bytes 589832 | tf_op jit(solution)/shard_map/ppermute | solution.py:1003
  38.0 7.5 %collective-permute-start.8 = (bf16[256,384]{1,0:T(8,128)(2,1)S(1)}, bf16[256,384]{1,0:T(8,128)(2,1)S(1)}, u32[]{:S(2)}, u32[]{:S(2)}) collective-permute-start(bf16[256,384]{1,0:T(8,128)(2,1)S(1)} %pack.1.refs_0_), channel_id=1, source_target_pairs={{0,4},{4,0},{8,12},{12,8},{16,20},{20,16},{24,28},{28,24},{1,5},{5... | collective-permute-start | bytes 589832 | tf_op jit(solution)/shard_map/ppermute | solution.py:980
  45.5 11.6 %collective-permute-start.4 = (bf16[3,128,512]{2,1,0:T(8,128)(2,1)S(1)}, bf16[3,128,512]{2,1,0:T(8,128)(2,1)S(1)}, u32[]{:S(2)}, u32[]{:S(2)}) collective-permute-start(bf16[3,128,512]{2,1,0:T(8,128)(2,1)S(1)} %slice.74), channel_id=1, source_target_pairs={{0,8},{4,12},{8,0},{12,4},{16,24},{20,28},{24,16},{28,20},{1,9},{5... | collective-permute-start | bytes 1179656 | tf_op jit(solution)/shard_map/ppermute | solution.py:980
  46.1 11.2 %collective-permute-start.5 = (bf16[3,128,512]{2,1,0:T(8,128)(2,1)S(1)}, bf16[3,128,512]{2,1,0:T(8,128)(2,1)S(1)}, u32[]{:S(2)}, u32[]{:S(2)}) collective-permute-start(bf16[3,128,512]{2,1,0:T(8,128)(2,1)S(1)} %slice.75), channel_id=1, source_target_pairs={{0,16},{4,20},{8,24},{12,28},{16,0},{20,4},{24,8},{28,12},{1,17},{... | collective-permute-start | bytes 1179656 | tf_op jit(solution)/shard_map/ppermute | solution.py:980
  58.1 14.5 %collective-permute-start.14 = (bf16[592,512]{1,0:T(8,128)(2,1)S(1)}, bf16[592,512]{1,0:T(8,128)(2,1)S(1)}, u32[]{:S(2)}, u32[]{:S(2)}) collective-permute-start(bf16[592,512]{1,0:T(8,128)(2,1)S(1)} %collective-permute-done.1.refs_1_), channel_id=1, source_target_pairs={{0,4},{4,0},{8,12},{12,8},{16,20},{20,16},{24,28},{28,24},{1,5},{5... | collective-permute-start | bytes 1818632 | tf_op jit(solution)/shard_map/ppermute | solution.py:980
  58.6 14.0 %collective-permute-start.13 = (bf16[592,512]{1,0:T(8,128)(2,1)S(1)}, bf16[592,512]{1,0:T(8,128)(2,1)S(1)}, u32[]{:S(2)}, u32[]{:S(2)}) collective-permute-start(bf16[592,512]{1,0:T(8,128)(2,1)S(1)} %pack_feed.1.refs_0_), channel_id=1, source_target_pairs={{0,4},{4,0},{8,12},{12,8},{16,20},{20,16},{24,28},{28,24},{1,5},{5... | collective-permute-start | bytes 1818632 | tf_op jit(solution)/shard_map/ppermute | solution.py:980
  59.4 13.3 %collective-permute-start.16 = (bf16[1,1024,256]{2,1,0:T(8,128)(2,1)S(1)}, bf16[1,1024,256]{2,1,0:T(8,128)(2,1)S(1)}, u32[]{:S(2)}, u32[]{:S(2)}) collective-permute-start(bf16[1,1024,256]{2,1,0:T(8,128)(2,1)S(1)} %get-tuple-element.150.refs_0_.refs_6_), channel_id=1, source_target_pairs={{0,4},{4,0},{8,12},{12,8},{16,20},{20,16},{24,28},{28,24},{1,5},{5... | collective-permute-start | bytes 1572872 | tf_op jit(solution)/shard_map/ppermute | solution.py:980
  59.9 21.6 %collective-permute-start.12 = (bf16[592,512]{1,0:T(8,128)(2,1)S(1)}, bf16[592,512]{1,0:T(8,128)(2,1)}, u32[]{:S(2)}, u32[]{:S(2)}) collective-permute-start(bf16[592,512]{1,0:T(8,128)(2,1)S(1)} %collective-permute-done.1.refs_1_), channel_id=1, source_target_pairs={{0,1},{1,2},{2,3},{3,0},{4,7},{5,4},{6,5},{7,6},{8,9},{9,10},{10,1... | collective-permute-start | bytes 1818632 | tf_op jit(solution)/shard_map/ppermute | solution.py:1003
  61.0 20.8 %collective-permute-start.18 = (bf16[1,1024,256]{2,1,0:T(8,128)(2,1)S(1)}, bf16[1,1024,256]{2,1,0:T(8,128)(2,1)S(1)}, u32[]{:S(2)}, u32[]{:S(2)}) collective-permute-start(bf16[1,1024,256]{2,1,0:T(8,128)(2,1)S(1)} %get-tuple-element.161.refs_0_.refs_6_), channel_id=1, source_target_pairs={{0,4},{4,0},{8,12},{12,8},{16,20},{20,16},{24,28},{28,24},{1,5},{5... | collective-permute-start | bytes 1572872 | tf_op jit(solution)/shard_map/ppermute | solution.py:980
  81.6 16.8 %collective-permute-start.17 = (bf16[592,512]{1,0:T(8,128)(2,1)}, bf16[592,512]{1,0:T(8,128)(2,1)}, u32[]{:S(2)}, u32[]{:S(2)}) collective-permute-start(bf16[592,512]{1,0:T(8,128)(2,1)} %collective-permute-done.12.refs_2_), channel_id=1, source_target_pairs={{0,1},{1,2},{2,3},{3,0},{4,7},{5,4},{6,5},{7,6},{8,9},{9,10},{10,1... | collective-permute-start | bytes 1818632 | tf_op jit(solution)/shard_map/ppermute | solution.py:1003
  93.2 18.2 %collective-permute-start.19 = (bf16[592,512]{1,0:T(8,128)(2,1)}, bf16[592,512]{1,0:T(8,128)(2,1)}, u32[]{:S(2)}, u32[]{:S(2)}) collective-permute-start(bf16[592,512]{1,0:T(8,128)(2,1)} %collective-permute-done.12.refs_2_), channel_id=1, source_target_pairs={{0,4},{4,0},{8,12},{12,8},{16,20},{20,16},{24,28},{28,24},{1,5},{5... | collective-permute-start | bytes 1818632 | tf_op jit(solution)/shard_map/ppermute | solution.py:980
  98.4 13.1 %collective-permute-start.20 = (bf16[592,512]{1,0:T(8,128)(2,1)}, bf16[592,512]{1,0:T(8,128)(2,1)}, u32[]{:S(2)}, u32[]{:S(2)}) collective-permute-start(bf16[592,512]{1,0:T(8,128)(2,1)} %collective-permute-done.17.refs_3_), channel_id=1, source_target_pairs={{0,4},{4,0},{8,12},{12,8},{16,20},{20,16},{24,28},{28,24},{1,5},{5... | collective-permute-start | bytes 1818632 | tf_op jit(solution)/shard_map/ppermute | solution.py:980
  98.4 8.0 %collective-permute-start.21 = (bf16[3,256,128]{2,1,0:T(8,128)(2,1)}, bf16[3,256,128]{2,1,0:T(8,128)(2,1)}, u32[]{:S(2)}, u32[]{:S(2)}) collective-permute-start(bf16[3,256,128]{2,1,0:T(8,128)(2,1)} %get-tuple-element.171), channel_id=1, source_target_pairs={{0,8},{4,12},{8,0},{12,4},{16,24},{20,28},{24,16},{28,20},{1,9},{5... | collective-permute-start | bytes 589832 | tf_op jit(solution)/shard_map/ppermute | solution.py:980
  99.9 11.6 %collective-permute-start.22 = (bf16[3,256,128]{2,1,0:T(8,128)(2,1)}, bf16[3,256,128]{2,1,0:T(8,128)(2,1)}, u32[]{:S(2)}, u32[]{:S(2)}) collective-permute-start(bf16[3,256,128]{2,1,0:T(8,128)(2,1)} %get-tuple-element.172), channel_id=1, source_target_pairs={{0,16},{4,20},{8,24},{12,28},{16,0},{20,4},{24,8},{28,12},{1,17},{... | collective-permute-start | bytes 589832 | tf_op jit(solution)/shard_map/ppermute | solution.py:980
  100.4 11.0 %collective-permute-start.23 = (bf16[3,256,128]{2,1,0:T(8,128)(2,1)}, bf16[3,256,128]{2,1,0:T(8,128)(2,1)}, u32[]{:S(2)}, u32[]{:S(2)}) collective-permute-start(bf16[3,256,128]{2,1,0:T(8,128)(2,1)} %get-tuple-element.173), channel_id=1, source_target_pairs={{0,24},{4,28},{8,16},{12,20},{16,8},{20,12},{24,0},{28,4},{1,25},{... | collective-permute-start | bytes 589832 | tf_op jit(solution)/shard_map/ppermute | solution.py:980
  141.2 7.6 %collective-permute-start.27 = (bf16[4,1,4,80,512]{4,3,2,1,0:T(8,128)(2,1)S(1)}, bf16[4,1,4,80,512]{4,3,2,1,0:T(8,128)(2,1)S(1)}, u32[]{:S(2)}, u32[]{:S(2)}) collective-permute-start(bf16[4,1,4,80,512]{4,3,2,1,0:T(8,128)(2,1)S(1)} %get-tuple-element.194), channel_id=1, source_target_pairs={{0,4},{4,0},{8,12},{12,8},{16,20},{20,16},{24,28},{28,24},{1,5},{5... | collective-permute-start | bytes 3932168 | tf_op jit(solution)/shard_map/ppermute | solution.py:980
  141.3 8.7 %collective-permute-start.24 = (bf16[3,256,128]{2,1,0:T(8,128)(2,1)S(1)}, bf16[3,256,128]{2,1,0:T(8,128)(2,1)S(1)}, u32[]{:S(2)}, u32[]{:S(2)}) collective-permute-start(bf16[3,256,128]{2,1,0:T(8,128)(2,1)S(1)} %copy-done.62), channel_id=1, source_target_pairs={{0,8},{4,12},{8,0},{12,4},{16,24},{20,28},{24,16},{28,20},{1,9},{5... | collective-permute-start | bytes 589832 | tf_op jit(solution)/shard_map/ppermute | solution.py:980
  141.9 11.3 %collective-permute-start.25 = (bf16[3,256,128]{2,1,0:T(8,128)(2,1)S(1)}, bf16[3,256,128]{2,1,0:T(8,128)(2,1)S(1)}, u32[]{:S(2)}, u32[]{:S(2)}) collective-permute-start(bf16[3,256,128]{2,1,0:T(8,128)(2,1)S(1)} %copy-done.61), channel_id=1, source_target_pairs={{0,16},{4,20},{8,24},{12,28},{16,0},{20,4},{24,8},{28,12},{1,17},{... | collective-permute-start | bytes 589832 | tf_op jit(solution)/shard_map/ppermute | solution.py:980
  143.1 11.5 %collective-permute-start.26 = (bf16[3,256,128]{2,1,0:T(8,128)(2,1)S(1)}, bf16[3,256,128]{2,1,0:T(8,128)(2,1)S(1)}, u32[]{:S(2)}, u32[]{:S(2)}) collective-permute-start(bf16[3,256,128]{2,1,0:T(8,128)(2,1)S(1)} %copy-done.60), channel_id=1, source_target_pairs={{0,24},{4,28},{8,16},{12,20},{16,8},{20,12},{24,0},{28,4},{1,25},{... | collective-permute-start | bytes 589832 | tf_op jit(solution)/shard_map/ppermute | solution.py:980
  148.8 19.3 %collective-permute-start.31 = (bf16[4,1,4,72,512]{4,3,2,1,0:T(8,128)(2,1)S(1)}, bf16[4,1,4,72,512]{4,3,2,1,0:T(8,128)(2,1)S(1)}, u32[]{:S(2)}, u32[]{:S(2)}) collective-permute-start(bf16[4,1,4,72,512]{4,3,2,1,0:T(8,128)(2,1)S(1)} %get-tuple-element.202), channel_id=1, source_target_pairs={{0,4},{4,0},{8,12},{12,8},{16,20},{20,16},{24,28},{28,24},{1,5},{5... | collective-permute-start | bytes 3538952 | tf_op jit(solution)/shard_map/ppermute | solution.py:980
  149.4 18.6 %collective-permute-start.28 = (bf16[1,4,80,512]{3,2,1,0:T(8,128)(2,1)S(1)}, bf16[1,4,80,512]{3,2,1,0:T(8,128)(2,1)S(1)}, u32[]{:S(2)}, u32[]{:S(2)}) collective-permute-start(bf16[1,4,80,512]{3,2,1,0:T(8,128)(2,1)S(1)} %get-tuple-element.196), channel_id=1, source_target_pairs={{0,8},{4,12},{8,0},{12,4},{16,24},{20,28},{24,16},{28,20},{1,9},{5... | collective-permute-start | bytes 983048 | tf_op jit(solution)/shard_map/ppermute | solution.py:980
  150.0 18.0 %collective-permute-start.29 = (bf16[1,4,80,512]{3,2,1,0:T(8,128)(2,1)S(1)}, bf16[1,4,80,512]{3,2,1,0:T(8,128)(2,1)S(1)}, u32[]{:S(2)}, u32[]{:S(2)}) collective-permute-start(bf16[1,4,80,512]{3,2,1,0:T(8,128)(2,1)S(1)} %get-tuple-element.197), channel_id=1, source_target_pairs={{0,16},{4,20},{8,24},{12,28},{16,0},{20,4},{24,8},{28,12},{1,17},{... | collective-permute-start | bytes 983048 | tf_op jit(solution)/shard_map/ppermute | solution.py:980
  153.2 14.8 %collective-permute-start.30 = (bf16[1,4,80,512]{3,2,1,0:T(8,128)(2,1)S(1)}, bf16[1,4,80,512]{3,2,1,0:T(8,128)(2,1)S(1)}, u32[]{:S(2)}, u32[]{:S(2)}) collective-permute-start(bf16[1,4,80,512]{3,2,1,0:T(8,128)(2,1)S(1)} %get-tuple-element.198), channel_id=1, source_target_pairs={{0,24},{4,28},{8,16},{12,20},{16,8},{20,12},{24,0},{28,4},{1,25},{... | collective-permute-start | bytes 983048 | tf_op jit(solution)/shard_map/ppermute | solution.py:980
  167.9 17.6 %collective-permute-start.35 = (bf16[1,1024,256]{2,1,0:T(8,128)(2,1)S(1)}, bf16[1,1024,256]{2,1,0:T(8,128)(2,1)S(1)}, u32[]{:S(2)}, u32[]{:S(2)}) collective-permute-start(bf16[1,1024,256]{2,1,0:T(8,128)(2,1)S(1)} %get-tuple-element.211), channel_id=1, source_target_pairs={{0,4},{4,0},{8,12},{12,8},{16,20},{20,16},{24,28},{28,24},{1,5},{5... | collective-permute-start | bytes 1572872 | tf_op jit(solution)/shard_map/ppermute | solution.py:980
  168.6 16.7 %collective-permute-start.32 = (bf16[1,4,72,512]{3,2,1,0:T(8,128)(2,1)S(1)}, bf16[1,4,72,512]{3,2,1,0:T(8,128)(2,1)S(1)}, u32[]{:S(2)}, u32[]{:S(2)}) collective-permute-start(bf16[1,4,72,512]{3,2,1,0:T(8,128)(2,1)S(1)} %get-tuple-element.204), channel_id=1, source_target_pairs={{0,8},{4,12},{8,0},{12,4},{16,24},{20,28},{24,16},{28,20},{1,9},{5... | collective-permute-start | bytes 884744 | tf_op jit(solution)/shard_map/ppermute | solution.py:980
  169.3 16.1 %collective-permute-start.33 = (bf16[1,4,72,512]{3,2,1,0:T(8,128)(2,1)S(1)}, bf16[1,4,72,512]{3,2,1,0:T(8,128)(2,1)S(1)}, u32[]{:S(2)}, u32[]{:S(2)}) collective-permute-start(bf16[1,4,72,512]{3,2,1,0:T(8,128)(2,1)S(1)} %get-tuple-element.205), channel_id=1, source_target_pairs={{0,16},{4,20},{8,24},{12,28},{16,0},{20,4},{24,8},{28,12},{1,17},{... | collective-permute-start | bytes 884744 | tf_op jit(solution)/shard_map/ppermute | solution.py:980
  170.8 14.7 %collective-permute-start.34 = (bf16[1,4,72,512]{3,2,1,0:T(8,128)(2,1)S(1)}, bf16[1,4,72,512]{3,2,1,0:T(8,128)(2,1)S(1)}, u32[]{:S(2)}, u32[]{:S(2)}) collective-permute-start(bf16[1,4,72,512]{3,2,1,0:T(8,128)(2,1)S(1)} %get-tuple-element.206), channel_id=1, source_target_pairs={{0,24},{4,28},{8,16},{12,20},{16,8},{20,12},{24,0},{28,4},{1,25},{... | collective-permute-start | bytes 884744 | tf_op jit(solution)/shard_map/ppermute | solution.py:980
  185.3 30.4 %collective-permute-start.40 = (bf16[1,1024,256]{2,1,0:T(8,128)(2,1)S(1)}, bf16[1,1024,256]{2,1,0:T(8,128)(2,1)S(1)}, u32[]{:S(2)}, u32[]{:S(2)}) collective-permute-start(bf16[1,1024,256]{2,1,0:T(8,128)(2,1)S(1)} %get-tuple-element.226), channel_id=1, source_target_pairs={{0,4},{4,0},{8,12},{12,8},{16,20},{20,16},{24,28},{28,24},{1,5},{5... | collective-permute-start | bytes 1572872 | tf_op jit(solution)/shard_map/ppermute | solution.py:980
  201.3 14.5 %collective-permute-start.41 = (bf16[1,1024,256]{2,1,0:T(8,128)(2,1)S(1)}, bf16[1,1024,256]{2,1,0:T(8,128)(2,1)S(1)}, u32[]{:S(2)}, u32[]{:S(2)}) collective-permute-start(bf16[1,1024,256]{2,1,0:T(8,128)(2,1)S(1)} %get-tuple-element.228), channel_id=1, source_target_pairs={{0,4},{4,0},{8,12},{12,8},{16,20},{20,16},{24,28},{28,24},{1,5},{5... | collective-permute-start | bytes 1572872 | tf_op jit(solution)/shard_map/ppermute | solution.py:980
  202.3 13.3 %collective-permute-start.39 = (bf16[2,152,512]{2,1,0:T(8,128)(2,1)S(1)}, bf16[2,152,512]{2,1,0:T(8,128)(2,1)S(1)}, u32[]{:S(2)}, u32[]{:S(2)}) collective-permute-start(bf16[2,152,512]{2,1,0:T(8,128)(2,1)S(1)} %bitcast.39), channel_id=1, source_target_pairs={{0,1},{1,0},{2,3},{3,2},{4,5},{5,4},{6,7},{7,6},{8,9},{9,8},{10,11... | collective-permute-start | bytes 933896 | tf_op jit(solution)/shard_map/ppermute | solution.py:1106
  202.3 8.1 %collective-permute-start.37 = (bf16[1,256,384]{2,1,0:T(8,128)(2,1)S(1)}, bf16[1,256,384]{2,1,0:T(8,128)(2,1)S(1)}, u32[]{:S(2)}, u32[]{:S(2)}) collective-permute-start(bf16[1,256,384]{2,1,0:T(8,128)(2,1)S(1)} %get-tuple-element.214), channel_id=1, source_target_pairs={{0,16},{4,20},{8,24},{12,28},{16,0},{20,4},{24,8},{28,12},{1,17},{... | collective-permute-start | bytes 589832 | tf_op jit(solution)/shard_map/ppermute | solution.py:980
  208.6 7.0 %collective-permute-start.38 = (bf16[1,256,384]{2,1,0:T(8,128)(2,1)S(1)}, bf16[1,256,384]{2,1,0:T(8,128)(2,1)S(1)}, u32[]{:S(2)}, u32[]{:S(2)}) collective-permute-start(bf16[1,256,384]{2,1,0:T(8,128)(2,1)S(1)} %get-tuple-element.215), channel_id=1, source_target_pairs={{0,24},{4,28},{8,16},{12,20},{16,8},{20,12},{24,0},{28,4},{1,25},{... | collective-permute-start | bytes 589832 | tf_op jit(solution)/shard_map/ppermute | solution.py:980
  218.2 13.9 %collective-permute-start.42 = (bf16[2,256,384]{2,1,0:T(8,128)(2,1)S(1)}, bf16[2,256,384]{2,1,0:T(8,128)(2,1)S(1)}, u32[]{:S(2)}, u32[]{:S(2)}) collective-permute-start(bf16[2,256,384]{2,1,0:T(8,128)(2,1)S(1)} %get-tuple-element.230), channel_id=1, source_target_pairs={{0,8},{4,12},{8,0},{12,4},{16,24},{20,28},{24,16},{28,20},{1,9},{5... | collective-permute-start | bytes 1179656 | tf_op jit(solution)/shard_map/ppermute | solution.py:980
  219.0 13.2 %collective-permute-start.43 = (bf16[2,256,384]{2,1,0:T(8,128)(2,1)S(1)}, bf16[2,256,384]{2,1,0:T(8,128)(2,1)S(1)}, u32[]{:S(2)}, u32[]{:S(2)}) collective-permute-start(bf16[2,256,384]{2,1,0:T(8,128)(2,1)S(1)} %get-tuple-element.231), channel_id=1, source_target_pairs={{0,16},{4,20},{8,24},{12,28},{16,0},{20,4},{24,8},{28,12},{1,17},{... | collective-permute-start | bytes 1179656 | tf_op jit(solution)/shard_map/ppermute | solution.py:980
  220.8 9.5 %collective-permute-start.44 = (bf16[152,512]{1,0:T(8,128)(2,1)S(1)}, bf16[152,512]{1,0:T(8,128)(2,1)S(1)}, u32[]{:S(2)}, u32[]{:S(2)}) collective-permute-start(bf16[152,512]{1,0:T(8,128)(2,1)S(1)} %get-tuple-element.233), channel_id=1, source_target_pairs={{0,2},{1,3},{2,0},{3,1},{4,6},{5,7},{6,4},{7,5},{8,10},{9,11},{10,... | collective-permute-start | bytes 466952 | tf_op jit(solution)/shard_map/ppermute | solution.py:1106
  221.6 10.5 %collective-permute-start.46 = (bf16[64,384]{1,0:T(8,128)(2,1)S(1)}, bf16[64,384]{1,0:T(8,128)(2,1)S(1)}, u32[]{:S(2)}, u32[]{:S(2)}) collective-permute-start(bf16[64,384]{1,0:T(8,128)(2,1)S(1)} %get-tuple-element.238), channel_id=1, source_target_pairs={{0,8},{4,12},{8,0},{12,4},{16,24},{20,28},{24,16},{28,20},{1,9},{5... | collective-permute-start | bytes 147464 | tf_op jit(solution)/shard_map/ppermute | solution.py:980
  222.7 9.5 %collective-permute-start.47 = (bf16[64,384]{1,0:T(8,128)(2,1)S(1)}, bf16[64,384]{1,0:T(8,128)(2,1)S(1)}, u32[]{:S(2)}, u32[]{:S(2)}) collective-permute-start(bf16[64,384]{1,0:T(8,128)(2,1)S(1)} %get-tuple-element.239), channel_id=1, source_target_pairs={{0,16},{4,20},{8,24},{12,28},{16,0},{20,4},{24,8},{28,12},{1,17},{... | collective-permute-start | bytes 147464 | tf_op jit(solution)/shard_map/ppermute | solution.py:980
  240.3 19.2 %collective-permute-start.49 = (bf16[2,256,384]{2,1,0:T(8,128)(2,1)S(1)}, bf16[2,256,384]{2,1,0:T(8,128)(2,1)S(1)}, u32[]{:S(2)}, u32[]{:S(2)}) collective-permute-start(bf16[2,256,384]{2,1,0:T(8,128)(2,1)S(1)} %get-tuple-element.242), channel_id=1, source_target_pairs={{0,24},{4,28},{8,16},{12,20},{16,8},{20,12},{24,0},{28,4},{1,25},{... | collective-permute-start | bytes 1179656 | tf_op jit(solution)/shard_map/ppermute | solution.py:980
  244.4 12.5 %collective-permute-start.55 = (bf16[200,512]{1,0:T(8,128)(2,1)S(1)}, bf16[200,512]{1,0:T(8,128)(2,1)S(1)}, u32[]{:S(2)}, u32[]{:S(2)}) collective-permute-start(bf16[200,512]{1,0:T(8,128)(2,1)S(1)} %total.1.refs_0_), channel_id=1, source_target_pairs={{0,24},{4,28},{8,16},{12,20},{16,8},{20,12},{24,0},{28,4},{1,25},{... | collective-permute-start | bytes 614408 | tf_op jit(solution)/shard_map/ppermute | solution.py:980
  245.4 13.6 %collective-permute-start.54 = (bf16[200,512]{1,0:T(8,128)(2,1)S(1)}, bf16[200,512]{1,0:T(8,128)(2,1)S(1)}, u32[]{:S(2)}, u32[]{:S(2)}) collective-permute-start(bf16[200,512]{1,0:T(8,128)(2,1)S(1)} %total.1.refs_0_), channel_id=1, source_target_pairs={{0,16},{4,20},{8,24},{12,28},{16,0},{20,4},{24,8},{28,12},{1,17},{... | collective-permute-start | bytes 614408 | tf_op jit(solution)/shard_map/ppermute | solution.py:980
  247.0 12.1 %collective-permute-start.53 = (bf16[200,512]{1,0:T(8,128)(2,1)S(1)}, bf16[200,512]{1,0:T(8,128)(2,1)S(1)}, u32[]{:S(2)}, u32[]{:S(2)}) collective-permute-start(bf16[200,512]{1,0:T(8,128)(2,1)S(1)} %total.1.refs_0_), channel_id=1, source_target_pairs={{0,8},{4,12},{8,0},{12,4},{16,24},{20,28},{24,16},{28,20},{1,9},{5... | collective-permute-start | bytes 614408 | tf_op jit(solution)/shard_map/ppermute | solution.py:980
  250.6 14.2 %collective-permute-start.56 = (bf16[200,512]{1,0:T(8,128)(2,1)S(1)}, bf16[200,512]{1,0:T(8,128)(2,1)S(1)}, u32[]{:S(2)}, u32[]{:S(2)}) collective-permute-start(bf16[200,512]{1,0:T(8,128)(2,1)S(1)} %total.1.refs_0_), channel_id=1, source_target_pairs={{0,4},{4,0},{8,12},{12,8},{16,20},{20,16},{24,28},{28,24},{1,5},{5... | collective-permute-start | bytes 614408 | tf_op jit(solution)/shard_map/ppermute | solution.py:980
  257.0 7.8 %collective-permute-start.59 = (bf16[200,512]{1,0:T(8,128)(2,1)S(1)}, bf16[200,512]{1,0:T(8,128)(2,1)S(1)}, u32[]{:S(2)}, u32[]{:S(2)}) collective-permute-start(bf16[200,512]{1,0:T(8,128)(2,1)S(1)} %collective-permute-done.55.refs_3_), channel_id=1, source_target_pairs={{0,4},{4,0},{8,12},{12,8},{16,20},{20,16},{24,28},{28,24},{1,5},{5... | collective-permute-start | bytes 614408 | tf_op jit(solution)/shard_map/ppermute | solution.py:980
  (75 other events, 598.9 us)
